TPU v7x, 128 devices: a whole 4x4x4 slice. The times are simulated.
128 devices in a mesh: member: 8 (over z, y_lo), band: 16 (over x, y_hi, core).
Axes of the slice: x: 4, y: 4 (y_hi: 2, y_lo: 2; y = y_hi * 2 + y_lo), z: 4, core: 2. Of those that a mesh axis runs over, the one named last changes fastest.
Arguments:
- hidden: bfloat16 [16, 1024, 1024], P('member', 'band'), may hold values from -6 to 6
- queries: bfloat16 [4096, 1024], P('band'), may hold values from -6 to 6
- kv_weight: bfloat16 [1024, 2048], replicated, may hold values from -0.1875 to 0.1875
- out_weight: bfloat16 [1024, 1024], replicated, may hold values from -0.1875 to 0.1875
- head_projection: bfloat16 [1024, 100], replicated, may hold values from -0.1875 to 0.1875
- initial_state: float32 [100, 4096], P(None, 'band'), may hold values from -6 to 6
- truth: float32 [100, 4096], P(None, 'band'), may hold values from -8 to 8
- latitude_weight: float32 [4096], P('band'), may hold values from 0.1 to 2
- channel_loss_weight: float32 [100], replicated, may hold values from 0.3 to 3
- sources: int32 [3, 4096], P(None, 'band'), may hold values from 0 to 127, as said below
- halo_rows: int32 [32, 32], P('band'), may hold values from 0 to 63, as said below
Outputs:
- hidden_grad: float32 [16, 1024, 1024], P('member', 'band')
- kv_grad: float32 [1024, 2048], P(('member', 'band'))
- out_grad: float32 [1024, 1024], P(('member', 'band'))
- head_grad: float32 [1024, 100], P(('member', 'band'))
Inputs may be any that keep to these rules, and one draw needn't show every extreme that they name: sources[e, t] names a row of the extended list of point t's band: rows below 64 are the band's own nodes, the next 32 those received from the band below, the last 32 those from the band above; the 3 rows of one point are distinct; the first band names no row from below and the last band none from above. `halo_rows`: rows 2 b and 2 b + 1 list the nodes of band b sent to the band below and to the band above; each node of a band stands once in the two rows together.
All inputs are finite; a program needn't handle non-finite values.
Results may differ from a plain program's by a relative error of at most 0.019.
Values may be sent and summed in bfloat16 or wider, within the bound.
A program may use at most 128 MiB of HBM per device.

v0:
```python
import jax
import jax.numpy as jnp
from jax import lax
from jax.sharding import PartitionSpec as P

HEAD_DIM = 64


ALPHA = 0.95
SOFTENING = 0.5


def padded(cells, sides, width):
    for axis, dim in sides:
        count = lax.axis_size(axis)
        ends = count - 1
        head = lax.slice_in_dim(cells, 0, width, axis=dim)
        tail = lax.slice_in_dim(cells, cells.shape[dim] - width, cells.shape[dim], axis=dim)
        cells = jnp.concatenate(
            [
                lax.ppermute(tail, axis, [(i, (i + 1) % count) for i in range(ends)]),
                cells,
                lax.ppermute(head, axis, [((i + 1) % count, i) for i in range(ends)]),
            ],
            axis=dim,
        )
    return cells


def ensemble_terms(local_rows, whole_ensemble, truth_part, lat_part, channel_loss_weight):
    members = whole_ensemble.shape[0]
    score_weight = channel_loss_weight[:, None] * lat_part[None, :]
    spread = (1.0 - (1.0 - ALPHA) / members) / (members * (members - 1))
    member_differences = local_rows[:, None] - whole_ensemble[None]
    gap_root = jnp.sqrt(member_differences * member_differences + SOFTENING * SOFTENING)
    slope_sum = jnp.sum(member_differences / gap_root, axis=1)
    truth_gap = local_rows - truth_part[None]
    truth_root = jnp.sqrt(truth_gap * truth_gap + SOFTENING * SOFTENING)
    return score_weight[None] * (truth_gap / truth_root / members - spread * slope_sum)


def shards(
    hidden,
    queries,
    kv_weight,
    out_weight,
    head_projection,
    initial_state,
    truth,
    latitude_weight,
    channel_loss_weight,
    sources,
    halo_rows,
):
    mem_count, node_count, model_width = hidden.shape
    grid_count = queries.shape[0]
    edge_count = sources.shape[0]
    head_count = model_width // HEAD_DIM
    score_scale = HEAD_DIM ** (-0.5)
    rim_size = halo_rows.shape[1]
    picked = jnp.stack([hidden[:, halo_rows[0]], hidden[:, halo_rows[1]]], axis=0)
    rim_rows = padded(picked, (("band", 0),), 1)
    extended_nodes = jnp.concatenate([hidden, rim_rows[0], rim_rows[3]], axis=1)
    ext_count = extended_nodes.shape[1]
    flat_ext = extended_nodes.reshape(mem_count * ext_count, model_width)
    key_value = jnp.dot(flat_ext, kv_weight, preferred_element_type=jnp.float32).astype(
        jnp.bfloat16
    )
    key_value = key_value.reshape(mem_count, ext_count, 2 * model_width)
    query_heads = queries.reshape(grid_count, head_count, HEAD_DIM)
    stored = []
    predictions = []
    for ensemble_member in range(mem_count):
        edge_rows = key_value[ensemble_member][sources]
        edge_keys = edge_rows[..., :model_width].reshape(
            edge_count, grid_count, head_count, HEAD_DIM
        )
        edge_messages = edge_rows[..., model_width:].reshape(
            edge_count, grid_count, head_count, HEAD_DIM
        )
        scores = (
            jnp.einsum("kthd,thd->kth", edge_keys, query_heads, preferred_element_type=jnp.float32)
            * score_scale
        )
        gate_activations = jax.nn.sigmoid(scores)
        gate_lowprecision = gate_activations.astype(jnp.bfloat16)
        combined_nodes = jnp.einsum(
            "kth,kthd->thd", gate_lowprecision, edge_messages, preferred_element_type=jnp.float32
        )
        combined_nodes = combined_nodes.reshape(grid_count, model_width).astype(jnp.bfloat16)
        updated = queries.astype(jnp.float32) + jnp.dot(
            combined_nodes, out_weight, preferred_element_type=jnp.float32
        )
        updated_lowprecision = updated.astype(jnp.bfloat16)
        prediction = initial_state + lax.dot_general(
            head_projection,
            updated_lowprecision,
            (((0,), (1,)), ((), ())),
            preferred_element_type=jnp.float32,
        )
        predictions.append(prediction)
        stored.append(
            (
                edge_messages,
                gate_activations,
                gate_lowprecision,
                combined_nodes,
                updated_lowprecision,
            )
        )
    local_prediction = jnp.stack(predictions, axis=0)
    whole_ensemble = lax.all_gather(local_prediction, "member", axis=0, tiled=True)
    loss_grad = ensemble_terms(
        local_prediction, whole_ensemble, truth, latitude_weight, channel_loss_weight
    )
    grad_rounded = loss_grad.astype(jnp.bfloat16)
    head_sum = jnp.zeros((model_width, head_projection.shape[1]), jnp.float32)
    out_sum = jnp.zeros((model_width, model_width), jnp.float32)
    node_grads = []
    for ensemble_member in range(mem_count):
        edge_messages, gate_activations, gate_lowprecision, combined_nodes, updated_lowprecision = (
            stored[ensemble_member]
        )
        member_grad = grad_rounded[ensemble_member]
        head_sum = head_sum + lax.dot_general(
            updated_lowprecision,
            member_grad,
            (((0,), (1,)), ((), ())),
            preferred_element_type=jnp.float32,
        )
        update_grad = lax.dot_general(
            member_grad,
            head_projection,
            (((0,), (1,)), ((), ())),
            preferred_element_type=jnp.float32,
        ).astype(jnp.bfloat16)
        out_sum = out_sum + lax.dot_general(
            combined_nodes,
            update_grad,
            (((0,), (0,)), ((), ())),
            preferred_element_type=jnp.float32,
        )
        merged_grad = lax.dot_general(
            update_grad, out_weight, (((1,), (1,)), ((), ())), preferred_element_type=jnp.float32
        ).astype(jnp.bfloat16)
        merged_grad = merged_grad.reshape(grid_count, head_count, HEAD_DIM)
        gate_grad = jnp.einsum(
            "thd,kthd->kth", merged_grad, edge_messages, preferred_element_type=jnp.float32
        )
        score_grad = gate_grad * gate_activations * (1.0 - gate_activations) * score_scale
        value_grad = (
            gate_lowprecision.astype(jnp.float32)[..., None] * merged_grad.astype(jnp.float32)[None]
        )
        key_grad = score_grad[..., None] * query_heads.astype(jnp.float32)[None]
        edge_grad = jnp.concatenate(
            [
                key_grad.reshape(edge_count, grid_count, model_width),
                value_grad.reshape(edge_count, grid_count, model_width),
            ],
            axis=-1,
        )
        node_sum = jax.ops.segment_sum(
            edge_grad.reshape(edge_count * grid_count, 2 * model_width),
            sources.reshape(-1),
            num_segments=ext_count,
        )
        node_grads.append(node_sum.astype(jnp.bfloat16))
    flat_node = jnp.stack(node_grads, axis=0).reshape(mem_count * ext_count, 2 * model_width)
    extended_grad = lax.dot_general(
        flat_node, kv_weight, (((1,), (1,)), ((), ())), preferred_element_type=jnp.float32
    )
    extended_grad = extended_grad.reshape(mem_count, ext_count, model_width)
    back_rows = jnp.stack(
        [
            extended_grad[:, node_count : node_count + rim_size],
            extended_grad[:, node_count + rim_size :],
        ],
        axis=0,
    )
    returned = padded(back_rows.astype(jnp.bfloat16), (("band", 0),), 1).astype(back_rows.dtype)
    hidden_grad = (
        extended_grad[:, :node_count]
        .at[:, halo_rows[0]]
        .add(returned[0])
        .at[:, halo_rows[1]]
        .add(returned[3])
    )
    devices = lax.axis_size("member") * lax.axis_size("band")
    kv_total = lax.psum_scatter(
        lax.dot_general(
            flat_ext, flat_node, (((0,), (0,)), ((), ())), preferred_element_type=jnp.float32
        ),
        ("member", "band"),
        scatter_dimension=0,
        tiled=True,
    )
    out_total, head_total = (
        lax.psum_scatter(out_sum, ("member", "band"), scatter_dimension=0, tiled=True),
        lax.psum_scatter(head_sum, ("member", "band"), scatter_dimension=0, tiled=True),
    )
    return (hidden_grad, kv_total / devices, out_total / devices, head_total / devices)


def solution(mesh):
    placed = (
        P("member", "band", None),
        P("band", None),
        P(),
        P(),
        P(),
        P(None, "band"),
        P(None, "band"),
        P("band"),
        P(),
        P(None, "band"),
        P("band", None),
    )
    return jax.shard_map(
        shards,
        mesh=mesh,
        in_specs=placed,
        out_specs=(
            P("member", "band", None),
            P(("member", "band"), None),
            P(("member", "band"), None),
            P(("member", "band"), None),
        ),
        check_vma=False,
    )
```

profile of v0, /device:TPU:1, one launch (start us, length us, event | category | flops | bytes accessed | tf_op | source)
XLA Modules:
  0.0 1571.4 jit_solution(14622490429388920891)
XLA Ops:
  11.2 6.2 collective-permute-start
  23.9 8.7 collective-permute-done.1
  35.1 3.4 convolution_convert_fusion
  38.6 4.3 gather_fusion.2
  42.9 4.1 fusion.40
  49.7 4.3 gather_fusion.3
  54.0 4.1 fusion.41
  76.7 45.3 %all-gather.2.cloned.1.call-done = f32[16,100,256]{2,1,0:T(8,128)} async-done(((f32[2,100,256]{2,1,0:T(8,128)}), f32[16,100,256]{2,1,0:T(8,128)}) %all-gather.2.cloned.1.call-update) | async-done | bytes 1638416 | tf_op jit(solution)/shard_map/all_gather | solution.py:112
  131.0 5.2 convolution_add_fusion
  145.7 3.9 copy.70
  152.5 3.6 copy.69
  163.2 3.6 copy.72
  169.7 3.7 copy.73
  173.4 4.5 bitcast_multiply_fusion.3
  182.1 3.5 bitcast_multiply_fusion.1
  185.5 16.3 %scatter_custom_fusion = f32[128,2048]{1,0:T(8,128)S(1)} fusion(s32[768]{0:T(1024)S(1)} %reshape.219, f32[768,1024]{1,0:T(8,128)} %bitcast_multiply_fusion.3, f32[]{:T(128)} %constant.42, f32[768,1024]{1,0:T(8,128)} %get-tuple-element.26, f32[]{:T(128)} %constant.10.clone.1), kind=kCustom, calls=%fused_computation.8 | custom fusion | flops 3145728 | bytes 7340040 | tf_op jit(solution)/shard_map/scatter-add | solution.py:162
  201.8 16.7 %scatter_custom_fusion.1 = f32[128,2048]{1,0:T(8,128)} fusion(s32[768]{0:T(1024)S(1)} %reshape.219, f32[768,1024]{1,0:T(8,128)} %bitcast_multiply_fusion.2, f32[]{:T(128)} %constant.42, f32[768,1024]{1,0:T(8,128)} %get-tuple-element.27, f32[]{:T(128)} %constant.10.clone.1), kind=kCustom, calls=%fused_computation.12 | custom fusion | flops 3145728 | bytes 7340040 | tf_op jit(solution)/shard_map/scatter-add | solution.py:162
  220.2 4.6 convolution_bitcast_fusion
  225.8 4.4 fusion.45
  230.2 5.1 collective-permute-start.2
  238.8 4.3 collective-permute-done.3
  248.7 26.9 %all-reduce.3.cloned.1.call-done = f32[1024,100]{1,0:T(8,128)} async-done(((f32[1024,100]{1,0:T(8,128)}), f32[1024,100]{1,0:T(8,128)}) %all-reduce.3.cloned.1.call-update) | async-done | bytes 409616
  276.9 637.5 %reduce-scatter.5.cloned.1.call-done = f32[8,1024]{1,0:T(8,128)} async-done(((f32[1024,1024]{1,0:T(8,128)}), f32[8,1024]{1,0:T(8,128)}) %reduce-scatter.5.cloned.1.call-update) | async-done | bytes 32784 | tf_op jit(solution)/shard_map/reduce_scatter | solution.py:198
  915.8 647.5 %reduce-scatter.3.cloned.1.call-done = f32[8,2048]{1,0:T(8,128)} async-done(((f32[1024,2048]{1,0:T(8,128)}), f32[8,2048]{1,0:T(8,128)}) %reduce-scatter.3.cloned.1.call-update) | async-done | bytes 65552 | tf_op jit(solution)/shard_map/reduce_scatter | solution.py:189
  (159 shorter events, 85.1 us)
Async XLA Ops:
  7.2 64.0 %copy-start = (bf16[1024,1024]{1,0:T(8,128)(2,1)S(1)}, bf16[1024,1024]{1,0:T(8,128)(2,1)}, u32[]{:S(2)}) copy-start(bf16[1024,1024]{1,0:T(8,128)(2,1)} %param.14) | copy-start | bytes 6291460
  7.2 15.0 copy-start.6
  7.2 114.7 %all-gather.2.cloned.1.call-start = ((), (), s32[]{:S(2)}) async-start(), calls=%async_computation.2 | async-start | bytes 1916928 | tf_op jit(solution)/shard_map/all_gather | solution.py:112
  8.1 15.4 copy-start.33
  8.1 15.4 copy-start.1
  11.2 12.7 collective-permute-start
  20.3 12.3 collective-permute-start.1
  63.8 5.5 copy-start.28
  66.5 4.7 copy-start.7
  72.4 3.5 copy-start.34
  72.4 3.5 copy-start.35
  75.7 199.9 %all-reduce.3.cloned.1.call-start = ((), (), s32[]{:S(2)}) async-start(), calls=%async_computation.5 | async-start | bytes 1048576
  122.0 4.7 copy-start.12
  125.6 4.2 copy-start.16
  130.9 783.4 %reduce-scatter.5.cloned.1.call-start = ((), (), s32[]{:S(2)}) async-start(), calls=%async_computation.4 | async-start | bytes 4227072 | tf_op jit(solution)/shard_map/reduce_scatter | solution.py:198
  136.2 1427.0 %reduce-scatter.3.cloned.1.call-start = ((), (), s32[]{:S(2)}) async-start(), calls=%async_computation.3 | async-start | bytes 8454144 | tf_op jit(solution)/shard_map/reduce_scatter | solution.py:189
  152.5 3.6 copy-start.15
  169.7 3.7 copy-start.18
  173.3 4.5 copy-start.3
  173.3 4.5 copy-start.19
  177.8 4.0 copy-start.5
  177.8 4.2 copy-start.21
  230.2 8.6 collective-permute-start.2
  235.4 7.8 collective-permute-start.3
  (20 other events, 39.7 us)
Sparse Core Ops, SparseCore 0:
  75.8 46.1 all-gather.1
  131.1 144.4 all-reduce.2
  278.1 636.2 reduce-scatter.4
  916.6 646.5 reduce-scatter.2
where the time goes:
time: 1590 us; the launch traced here: 1570 us
  waiting for transfers between devices  1370 us (86%)
  local copies, waits for them, and re-layouts  72 us (5%)
  other arithmetic  69.8 us (4%)
  matrix products  29.1 us (2%)
    reduce_scatter x1, waiting for transfers between devices, shards(): lax.psum_scatter(lax.dot_general(flat_ext, flat_node, (((0,), (0,)), ((),...  647 us
    reduce_scatter x1, waiting for transfers between devices, shards(): lax.psum_scatter(out_sum, ('member', 'band'), scatter_dimension=0, tiled=...  638 us
    all_gather x1, waiting for transfers between devices, shards(): lax.all_gather(local_prediction, 'member', axis=0, tiled=True)  45.3 us
    scatter-add x2, other arithmetic, shards(): jax.ops.segment_sum(edge_grad.reshape(edge_count * grid_count, 2 * model_...  33 us
  transfers between devices with their start and end apart: 8, of which 6 were waited for; matrix products, arithmetic and copies ran while one was open for 7% of the time, Pallas kernels for 0%

commit v1 on v0

v1 whole, which is shorter than its diff:
```python
import jax
import jax.numpy as jnp
from jax import lax
from jax.experimental import pallas as pl
from jax.experimental.pallas import tpu as pltpu
from jax.sharding import PartitionSpec as P

MESH = pl.DeviceIdType.MESH
BF = jnp.bfloat16
F32 = jnp.float32
ALPHA = 0.95
SOFTENING = 0.5
MEMBERS = 16
DEVICES = 128
NN = (((1,), (0,)), ((), ()))
NT = (((1,), (1,)), ((), ()))


def mm(a, b, dims=NN):
    return lax.dot_general(a, b, dims, preferred_element_type=F32)


def body(
    hid_hbm, q_hbm, kvw_hbm, ow_hbm, head, init, truth, lat, cw, src, halo,
    hg_out, kv_out, og_out, hd_out,
    ext, q3, kvw, ow, owt, qt, headp, headt, hgt, pick, lrow, kv3, mask, gt, dsg, um,
    initp, truthp, wts, f3, fg, lloc, l4, ug, dm, ah, ahr, nown, nsend, nrecv, nsnd, nrcv, nt,
    kvp, kvr, fsnd, frcv,
    in_sem, halo_s, halo_r, hid_s, hid_r, fc_s, fc_r, lg_s, lg_r, ah_s, ah_r, nh_s, nh_r,
    na_s, na_r, rs_s, rs_r, fin_s, fin_r,
):
    mem, band = lax.axis_index("member"), lax.axis_index("band")
    z, ylo = mem // 2, mem % 2
    core = band % 2
    group = z * 2 + core
    plane = ylo * 8 + band // 2

    def group_peer(j):
        return (j // 2) * 2 + ylo, band - core + j % 2

    def plane_peer(q):
        return z * 2 + q // 8, (q % 8) * 2 + core

    def member_peer(m):
        return m, band

    below, above = (mem, (band + 15) % 16), (mem, (band + 1) % 16)

    def each(count, fn):
        def step(k, carry):
            fn(k)
            return carry
        lax.fori_loop(1, count, step, 0)

    def remote(source, target, send, recv, device):
        return pltpu.make_async_remote_copy(
            src_ref=source, dst_ref=target, send_sem=send, recv_sem=recv,
            device_id=device, device_id_type=MESH)

    loads = [pltpu.make_async_copy(hid_hbm, ext.at[:, 0:2], in_sem.at[0]),
             pltpu.make_async_copy(kvw_hbm, kvw, in_sem.at[1]),
             pltpu.make_async_copy(ow_hbm, ow, in_sem.at[2])]
    loads += [pltpu.make_async_copy(q_hbm.at[:, 128 * p:128 * p + 128], q3.at[p], in_sem.at[3 + p])
              for p in range(8)]
    for copy in loads:
        copy.start()

    barrier = pltpu.get_barrier_semaphore()

    def greet(device):
        pl.semaphore_signal(barrier, inc=1, device_id=device, device_id_type=MESH)

    greet(below)
    greet(above)
    each(8, lambda k: greet(group_peer((group + k) % 8)))
    each(8, lambda k: greet(member_peer((mem + k) % 8)))
    each(16, lambda k: greet(plane_peer((plane + k) % 16)))

    for m in range(2):
        for d in range(2):
            at = 64 * m + 32 * d
            lrow[0:1, at:at + 32] = halo[d:d + 1, :] + 64 * m
    row_of = lax.broadcasted_iota(jnp.int32, (128, 128), 0)
    lane_of = lax.broadcasted_iota(jnp.int32, (128, 128), 1)
    scatter = (row_of == lrow[0:1, :]).astype(F32)
    gather = scatter.T.astype(BF)
    scatter = scatter.astype(BF)

    loads[0].wait()
    own = ext[:, 0:2].reshape(128, 1024)
    for n in range(4):
        cols = slice(256 * n, 256 * n + 256)
        pick[:, :, :, cols] = mm(gather, own[:, cols]).astype(BF).reshape(2, 2, 32, 256)

    pl.semaphore_wait(barrier, 31)
    to_below = remote(pick.at[:, 0], ext.at[:, 3], halo_s.at[0], halo_r.at[0], below)
    to_above = remote(pick.at[:, 1], ext.at[:, 2], halo_s.at[1], halo_r.at[1], above)
    to_below.start()
    to_above.start()

    mine = pl.ds(pl.multiple_of(group * 128, 128), 128)
    for n in range(8):
        rows = slice(128 * n, 128 * n + 128)
        hgt[rows, mine] = own[:, rows].T

    def hid_copy(k):
        return remote(hgt.at[:, mine], hgt.at[:, mine], hid_s.at[k], hid_r.at[k],
                      group_peer((group + k) % 8))

    each(8, lambda k: hid_copy(k).start())

    headp[...] = jnp.zeros_like(headp)
    headp[:, 0:100] = head[...]
    headt[...] = headp[...].T
    initp[...] = jnp.zeros_like(initp)
    initp[0:100, :] = init[...]
    truthp[...] = jnp.zeros_like(truthp)
    truthp[0:100, :] = truth[...]
    lrow[1:2, :] = jnp.zeros_like(lrow[1:2, :])
    diag = jnp.where(row_of == lane_of, cw[...], 0.0)
    wts[...] = jnp.sum(diag, axis=1, keepdims=True) * lat[...]
    point_row = lax.broadcasted_iota(jnp.int32, (128, 256), 0)
    edge = (point_row == src[0:1, :]) | (point_row == src[1:2, :]) | (point_row == src[2:3, :])
    mask[0:128, :] = edge.astype(F32)
    mask[128:256, :] = edge.astype(F32)
    lo_lane = (lane_of < 64).astype(BF)
    hi_lane = (lane_of >= 64).astype(BF)
    lo_row = (row_of < 64).astype(BF)
    hi_row = (row_of >= 64).astype(BF)
    for p in range(8):
        loads[3 + p].wait()
        qt[128 * p:128 * p + 128, :] = q3[p].T
    loads[2].wait()
    for i in range(4):
        rows = slice(256 * i, 256 * i + 256)
        for j in range(4):
            cols = slice(256 * j, 256 * j + 256)
            owt[rows, cols] = ow[cols, rows].T

    loads[1].wait()
    to_below.wait_recv()
    to_above.wait_recv()
    rows256 = ext[...].reshape(256, 1024)
    for n in range(8):
        part = mm(rows256, kvw[:, 256 * n:256 * n + 256]).astype(BF)
        kv3[2 * n] = part[:, :128]
        kv3[2 * n + 1] = part[:, 128:]

    def forward(p, carry):
        for m in range(2):
            kp = kv3[p, 128 * m:128 * m + 128, :]
            vt = kv3[8 + p, 128 * m:128 * m + 128, :].T
            kcat = jnp.concatenate([kp * lo_lane, kp * hi_lane], axis=0)
            score = mm(kcat, q3[p], NT)
            th = jnp.tanh(score * (0.5 / 8.0))
            on = mask[...]
            gate = ((0.5 + 0.5 * th) * on).astype(BF)
            gt[m, p] = gate
            dsg[m, p] = (0.25 - 0.25 * th * th) * (on * 0.125)
            vcat_t = jnp.concatenate([vt * lo_row, vt * hi_row], axis=1)
            um[m, pl.ds(pl.multiple_of(p * 128, 128), 128), :] = mm(vcat_t, gate).astype(BF)
        return carry

    lax.fori_loop(0, 8, forward, 0)

    for m in range(2):
        merged = um[m, 0:1024, :]
        for i in range(4):
            rows = slice(256 * i, 256 * i + 256)
            up = mm(owt[rows, :], merged) + qt[rows, :].astype(F32)
            um[m, 1024 + 256 * i:1024 + 256 * i + 256, :] = up.astype(BF)
        f3[m] = mm(headt[...], um[m, 1024:2048, :]) + initp[...]

    def fc_copy(k):
        to = (mem + k) % 8
        return remote(f3.at[:, pl.ds(pl.multiple_of(to * 16, 16), 16), :], fg.at[pl.ds(2 * mem, 2)],
                      fc_s.at[k], fc_r.at[k], member_peer(to))

    each(8, lambda k: fc_copy(k).start())
    my_rows = pl.ds(pl.multiple_of(mem * 16, 16), 16)
    for m in range(2):
        fg[2 * mem + m] = f3[m, my_rows, :]
    each(8, lambda k: remote(f3.at[:, my_rows, :], fg.at[pl.ds(2 * ((mem + 8 - k) % 8), 2)],
                             fc_s.at[k], fc_r.at[k], member_peer((mem + k) % 8)).wait_recv())

    spread = (1.0 - (1.0 - ALPHA) / MEMBERS) / (MEMBERS * (MEMBERS - 1))
    soft = SOFTENING * SOFTENING
    truth_rows = truthp[my_rows, :]
    weight = wts[my_rows, :]

    def loss(m, carry):
        f = fg[m]
        gap = f[None] - fg[...]
        slopes = jnp.sum(gap * lax.rsqrt(gap * gap + soft), axis=0)
        off = f - truth_rows
        slope = off * lax.rsqrt(off * off + soft)
        lloc[m] = (weight * (slope * (1.0 / MEMBERS) - spread * slopes)).astype(BF)
        return carry

    lax.fori_loop(0, MEMBERS, loss, 0)

    def lg_copy(k):
        to = (mem + k) % 8
        return remote(lloc.at[pl.ds(2 * to, 2)], l4.at[:, mem], lg_s.at[k], lg_r.at[k],
                      member_peer(to))

    each(8, lambda k: lg_copy(k).start())
    for m in range(2):
        l4[m, mem] = lloc[2 * mem + m]
    each(8, lambda k: remote(lloc.at[pl.ds(2 * mem, 2)], l4.at[:, (mem + 8 - k) % 8],
                             lg_s.at[k], lg_r.at[k], member_peer((mem + k) % 8)).wait_recv())

    for m in range(2):
        grad = l4[m].reshape(128, 256)
        for i in range(4):
            rows = slice(256 * i, 256 * i + 256)
            ug[m, rows, :] = mm(headp[rows, :], grad).astype(BF)
        for i in range(4):
            rows = slice(256 * i, 256 * i + 256)
            dm[m, rows, :] = mm(ow[rows, :], ug[m]).astype(BF)

    low = lane_of < 64

    def backward(p, carry):
        for m in range(2):
            vp = kv3[8 + p, 128 * m:128 * m + 128, :]
            vcat = jnp.concatenate([vp * lo_lane, vp * hi_lane], axis=0)
            grad = dm[m, pl.ds(pl.multiple_of(p * 128, 128), 128), :]
            score_grad = (mm(vcat, grad) * dsg[m, p]).astype(BF)
            dk = mm(score_grad, q3[p])
            dv = mm(gt[m, p], grad, NT)
            for c, both in ((p, dk), (8 + p, dv)):
                rows = jnp.where(low, both[:128], both[128:])
                nown[c, 64 * m:64 * m + 64, :] = rows[0:64]
                nsend[0, c, m] = rows[64:96].astype(BF)
                nsend[1, c, m] = rows[96:128].astype(BF)
        return carry

    lax.fori_loop(0, 8, backward, 0)
    back_below = remote(nsend.at[0], nrecv.at[:, :, 1], nh_s.at[0], nh_r.at[0], below)
    back_above = remote(nsend.at[1], nrecv.at[:, :, 0], nh_s.at[1], nh_r.at[1], above)
    back_below.start()
    back_above.start()

    for a in range(2):
        for i in range(4):
            rows = slice(1024 * a + 256 * i, 1024 * a + 256 * i + 256)
            both = mm(um[0, rows, :], l4[0].reshape(128, 256), NT) + mm(
                um[1, rows, :], l4[1].reshape(128, 256), NT)
            ah[a, i] = both.astype(BF).reshape(16, 16, 128)

    def ah_copy(k):
        to = (plane + k) % 16
        return remote(ah.at[:, :, to], ahr.at[plane], ah_s.at[k], ah_r.at[k], plane_peer(to))

    each(16, lambda k: ah_copy(k).start())
    ahr[plane] = ah[:, :, plane]

    back_below.wait_recv()
    back_above.wait_recv()
    for c in range(16):
        total = nown[c] + mm(scatter, nrecv[c].reshape(128, 128))
        rounded = total.astype(BF)
        nt[:, 128 * c:128 * c + 128] = rounded
        nsnd[c // 2, :, 128 * (c % 2):128 * (c % 2) + 128] = rounded

    def na_copy(k):
        to = (group + k) % 8
        return remote(nsnd.at[to], nrcv.at[group], na_s.at[k], na_r.at[k], group_peer(to))

    each(8, lambda k: na_copy(k).start())
    nrcv[group] = nsnd[group]

    for i in range(4):
        rows = slice(256 * i, 256 * i + 256)
        hg_out[:, rows] = mm(nt[...], kvw[rows, :], NT)

    each(8, lambda k: remote(hgt.at[:, mine], hgt.at[:, pl.ds(pl.multiple_of(((group + 8 - k) % 8) * 128, 128), 128)],
                             hid_s.at[k], hid_r.at[k], group_peer((group + k) % 8)).wait_recv())
    each(8, lambda k: remote(nsnd.at[group], nrcv.at[(group + 8 - k) % 8], na_s.at[k], na_r.at[k],
                             group_peer((group + k) % 8)).wait_recv())
    cols256 = nrcv[...].reshape(1024, 256)
    for i in range(4):
        rows = slice(256 * i, 256 * i + 256)
        kvp[i] = mm(hgt[rows, :], cols256).astype(BF).reshape(16, 16, 256)

    def rs_copy(k):
        to = (plane + k) % 16
        return remote(kvp.at[:, to], kvr.at[plane], rs_s.at[k], rs_r.at[k], plane_peer(to))

    each(16, lambda k: rs_copy(k).start())
    kvr[plane] = kvp[:, plane]

    each(16, lambda k: remote(ah.at[:, :, plane], ahr.at[(plane + 16 - k) % 16], ah_s.at[k], ah_r.at[k],
                              plane_peer((plane + k) % 16)).wait_recv())
    ah_sum = jnp.sum(ahr[...].astype(F32), axis=0)
    fsnd[:, 8:16, 0:128] = ah_sum[0].reshape(8, 8, 128)
    fsnd[:, 8:16, 128:256] = ah_sum[1].reshape(8, 8, 128)
    each(16, lambda k: remote(kvp.at[:, plane], kvr.at[(plane + 16 - k) % 16], rs_s.at[k], rs_r.at[k],
                              plane_peer((plane + k) % 16)).wait_recv())
    fsnd[:, 0:8, :] = jnp.sum(kvr[...].astype(F32), axis=0).reshape(8, 8, 256)

    def fin_copy(k):
        to = (group + k) % 8
        return remote(fsnd.at[to], frcv.at[group], fin_s.at[k], fin_r.at[k], group_peer(to))

    each(8, lambda k: fin_copy(k).start())
    frcv[group] = fsnd[group]
    each(8, lambda k: remote(fsnd.at[group], frcv.at[(group + 8 - k) % 8], fin_s.at[k], fin_r.at[k],
                             group_peer((group + k) % 8)).wait_recv())
    for j in range(8):
        kv_out[:, 256 * j:256 * j + 256] = frcv[j, 0:8, :] * (1.0 / DEVICES)
    sums = jnp.sum(frcv[:, 8:16, :], axis=0) * (1.0 / DEVICES)
    hd_out[...] = sums[:, 128:228]
    outer = sums[:, 0:128]
    big = outer.astype(BF)
    small = (outer - big.astype(F32)).astype(BF)
    og_out[...] = mm(big, headt[...]) + mm(small, headt[...])

    to_below.wait_send()
    to_above.wait_send()
    back_below.wait_send()
    back_above.wait_send()
    for count, copy in ((8, hid_copy), (8, fc_copy), (8, lg_copy), (8, na_copy), (8, fin_copy),
                        (16, ah_copy), (16, rs_copy)):
        each(count, lambda k, copy=copy: copy(k).wait_send())


def shards(hidden, queries, kv_weight, out_weight, head_projection, initial_state, truth,
           latitude_weight, channel_loss_weight, sources, halo_rows):
    vmem = pl.BlockSpec(memory_space=pltpu.VMEM)
    hbm = pl.BlockSpec(memory_space=pl.ANY)
    dma = pltpu.SemaphoreType.DMA
    scratch = [
        ((2, 4, 32, 1024), BF), ((8, 256, 128), BF), ((1024, 2048), BF), ((1024, 1024), BF),
        ((1024, 1024), BF), ((1024, 256), BF), ((1024, 128), BF), ((128, 1024), BF),
        ((1024, 1024), BF), ((2, 2, 32, 1024), BF), ((8, 128), jnp.int32), ((16, 256, 128), BF),
        ((256, 256), F32), ((2, 8, 256, 256), BF), ((2, 8, 256, 256), F32), ((2, 2048, 256), BF),
        ((128, 256), F32), ((128, 256), F32), ((128, 256), F32), ((2, 128, 256), F32),
        ((16, 16, 256), F32), ((16, 16, 256), BF), ((2, 8, 16, 256), BF), ((2, 1024, 256), BF),
        ((2, 1024, 256), BF), ((2, 4, 16, 16, 128), BF), ((16, 2, 4, 16, 128), BF),
        ((16, 128, 128), F32), ((2, 16, 2, 32, 128), BF), ((16, 2, 2, 32, 128), BF),
        ((8, 128, 256), BF), ((8, 128, 256), BF), ((128, 2048), BF), ((4, 16, 16, 256), BF),
        ((16, 4, 16, 256), BF), ((8, 16, 256), F32), ((8, 16, 256), F32),
    ]
    sems = [11, 2, 2, 8, 8, 8, 8, 8, 8, 16, 16, 2, 2, 8, 8, 16, 16, 8, 8]
    hidden_grad, kv_grad, out_grad, head_grad = pl.pallas_call(
        body,
        out_shape=[jax.ShapeDtypeStruct((128, 1024), F32), jax.ShapeDtypeStruct((8, 2048), F32),
                   jax.ShapeDtypeStruct((8, 1024), F32), jax.ShapeDtypeStruct((8, 100), F32)],
        in_specs=[hbm] * 4 + [vmem] * 7,
        out_specs=[vmem] * 4,
        scratch_shapes=[pltpu.VMEM(shape, kind) for shape, kind in scratch] + [dma((n,)) for n in sems],
        compiler_params=pltpu.CompilerParams(
            collective_id=0, has_side_effects=True, vmem_limit_bytes=56 * 1024 * 1024),
    )(
        hidden.reshape(2, 2, 32, 1024), queries, kv_weight, out_weight, head_projection,
        initial_state, truth, latitude_weight.reshape(1, 256),
        jnp.pad(channel_loss_weight, (0, 28)).reshape(1, 128), sources, halo_rows,
    )
    return hidden_grad.reshape(2, 64, 1024), kv_grad, out_grad, head_grad


def solution(mesh):
    placed = (
        P("member", "band", None),
        P("band", None),
        P(),
        P(),
        P(),
        P(None, "band"),
        P(None, "band"),
        P("band"),
        P(),
        P(None, "band"),
        P("band", None),
    )
    return jax.shard_map(
        shards,
        mesh=mesh,
        in_specs=placed,
        out_specs=(
            P("member", "band", None),
            P(("member", "band"), None),
            P(("member", "band"), None),
            P(("member", "band"), None),
        ),
        check_vma=False,
    )
```

time: 1590 us -> 93.6 us (0.06); the launches traced: 1570 us -> 93.3 us
  waiting for transfers between devices: 1370 us -> 0 us
  Pallas kernels: 0 us -> 83.7 us
  other arithmetic: 69.8 us -> 0 us
  local copies, waits for them, and re-layouts: 72 us -> 8.95 us
  matrix products: 29.1 us -> 0 us
    reduce_scatter x2 -> x0, waiting for transfers between devices: 1280 us -> none  [the longest x1 647 us: shards(): lax.psum_scatter(lax.dot_general(flat_ext, flat_node, (((0,), (0,)), ((),...]
    pallas_call x0 -> x1, Pallas kernels: none -> 83.7 us  [shards(): pl.pallas_call(body, out_shape=[jax.ShapeDtypeStruct((128, 1024), F32), j...]
    all_gather x1 -> x0, waiting for transfers between devices: 45.3 us -> none  [shards(): lax.all_gather(local_prediction, 'member', axis=0, tiled=True)]
    scatter-add x4 -> x0, other arithmetic: 37 us -> none  [the longest x2 33 us: shards(): jax.ops.segment_sum(edge_grad.reshape(edge_count * grid_count, 2 * model_...]
    dot_general x15 -> x0, matrix products: 29.1 us -> none  [the longest x2 7.91 us: shards(): lax.dot_general(combined_nodes, update_grad, (((0,), (0,)), ((), ())), pr...]
    unnamed x5 -> x0, waiting for transfers between devices: 27 us -> none
    unnamed x85 -> x5, local copies, waits for them, and re-layouts: 26.7 us -> 7.79 us
    mul x8 -> x0, local copies, waits for them, and re-layouts: 16.8 us -> none  [the longest x4 8.61 us: shards(): gate_lowprecision.astype(jnp.float32)[..., None]]
  transfers between devices with their start and end apart: 8 -> 0, of which waited for: 6 -> 0; matrix products, arithmetic and copies ran while one was open for 7% -> 0% of each run, Pallas kernels for 0% -> 0%
where the time goes in v1:
time: 93.6 us; the launch traced here: 93.3 us
  Pallas kernels  83.7 us (89%)
  local copies, waits for them, and re-layouts  8.95 us (10%)
    pallas_call x1, Pallas kernels, shards(): pl.pallas_call(body, out_shape=[jax.ShapeDtypeStruct((128, 1024), F32), j...  83.7 us
    unnamed x5, local copies, waits for them, and re-layouts  7.79 us

profile of v1, /device:TPU:1, one launch (start us, length us, event | category | flops | bytes accessed | tf_op | source)
XLA Modules:
  0.0 93.3 jit_solution(3569754905258212841)
XLA Ops:
  0.6 1.2 %pad_bitcast_fusion.cw = f32[1,128]{1,0:T(1,128)} fusion(f32[100]{0:T(128)} %param.19), kind=kLoop, calls=%fused_computation | loop fusion | bytes 912 | tf_op jit(solution)/shard_map/reshape | solution.py:359
  1.8 1.8 %copy.15.head = bf16[1024,100]{1,0:T(8,128)(2,1)} copy(bf16[1024,100]{0,1:T(8,128)(2,1)} %param.15) | data formatting | bytes 409600 | tf_op args[4]
  3.6 83.7 %shard_map.138 = (f32[128,1024]{1,0:T(8,128)}, f32[8,2048]{1,0:T(8,128)}, f32[8,1024]{1,0:T(8,128)}, f32[8,100]{1,0:T(8,128)}) custom-call(bf16[2,2,32,1024]{3,2,1,0:T(8,128)(2,1)} %bitcast.6, bf16[256,1024]{1,0:T(8,128)(2,1)} %q_hbm.1, bf16[1024,2048]{1,0:T(8,128)(2,1)} %kvw_hbm.1, bf16[1024,1024]{1,0:T(8,128)(2,1)} %ow_hbm.1, ...), custom_call_target="tpu_custom_call" | custom-call | tf_op jit(solution)/shard_map/pallas_call | solution.py:347
  87.3 1.9 %copy.20 = f32[2,64,1024]{2,1,0:T(8,128)} copy(f32[2,64,1024]{2,1,0:T(8,128)} %bitcast.5) | data formatting | bytes 1048576
  89.1 1.5 %copy.21 = f32[8,2048]{1,0:T(8,128)} copy(f32[8,2048]{1,0:T(8,128)} %get-tuple-element.17) | data formatting | bytes 131072
  90.6 1.4 %copy.22 = f32[8,1024]{1,0:T(8,128)} copy(f32[8,1024]{1,0:T(8,128)} %get-tuple-element.18) | data formatting | bytes 65536
  92.0 1.3 %copy.23 = f32[8,100]{1,0:T(8,128)} copy(f32[8,100]{1,0:T(8,128)} %get-tuple-element.19) | data formatting | bytes 6400

commit v2 on v1

--- a/solution.py
+++ b/solution.py
@@ -22,12 +22,12 @@
 
 def body(
     hid_hbm, q_hbm, kvw_hbm, ow_hbm, head, init, truth, lat, cw, src, halo,
-    hg_out, kv_out, og_out, hd_out,
-    ext, q3, kvw, ow, owt, qt, headp, headt, hgt, pick, lrow, kv3, mask, gt, dsg, um,
-    initp, truthp, wts, f3, fg, lloc, l4, ug, dm, ah, ahr, nown, nsend, nrecv, nsnd, nrcv, nt,
-    kvp, kvr, fsnd, frcv,
-    in_sem, halo_s, halo_r, hid_s, hid_r, fc_s, fc_r, lg_s, lg_r, ah_s, ah_r, nh_s, nh_r,
-    na_s, na_r, rs_s, rs_r, fin_s, fin_r,
+    hg_hbm, frcv, headt,
+    ext, q3, kvw, ow, owt, qt, headp, hgt, pick, lrow, kv3, mask, gt, dsg, um,
+    initp, truthp, wts, f3, fg, lloc, l4, ug, dm, ah, ahx, ahs, ahr, nown, nsend, nrecv, nsnd, nrcv, nt,
+    kvp, kvr, fsnd, hg,
+    in_sem, out_sem, halo_s, halo_r, hid_s, hid_r, sib_s, sib_r, fc_s, fc_r, lg_s, lg_r, ah_s, ah_r, nh_s, nh_r,
+    na_s, na_r, rs_s, rs_r, fin_s, fin_r, ax_s, ax_r,
 ):
     mem, band = lax.axis_index("member"), lax.axis_index("band")
     z, ylo = mem // 2, mem % 2
@@ -44,6 +44,10 @@
     def member_peer(m):
         return m, band
 
+    pending = []
+
+    sib_group = group + 1 - 2 * core
+    sibling = (mem, band + 1 - 2 * core)
     below, above = (mem, (band + 15) % 16), (mem, (band + 1) % 16)
 
     def each(count, fn):
@@ -73,7 +77,8 @@
     greet(below)
     greet(above)
     each(8, lambda k: greet(group_peer((group + k) % 8)))
-    each(8, lambda k: greet(member_peer((mem + k) % 8)))
+    for k in range(4):
+        greet(member_peer((mem + 2 * k + 1) % 8))
     each(16, lambda k: greet(plane_peer((plane + k) % 16)))
 
     for m in range(2):
@@ -92,32 +97,53 @@
         cols = slice(256 * n, 256 * n + 256)
         pick[:, :, :, cols] = mm(gather, own[:, cols]).astype(BF).reshape(2, 2, 32, 256)
 
-    pl.semaphore_wait(barrier, 31)
+    pl.semaphore_wait(barrier, 28)
     to_below = remote(pick.at[:, 0], ext.at[:, 3], halo_s.at[0], halo_r.at[0], below)
     to_above = remote(pick.at[:, 1], ext.at[:, 2], halo_s.at[1], halo_r.at[1], above)
     to_below.start()
     to_above.start()
+    pending.append((1, lambda k: to_below))
+    pending.append((1, lambda k: to_above))
 
     mine = pl.ds(pl.multiple_of(group * 128, 128), 128)
     for n in range(8):
         rows = slice(128 * n, 128 * n + 128)
         hgt[rows, mine] = own[:, rows].T
 
+    def hid_columns(j):
+        return hgt.at[:, pl.ds(pl.multiple_of(j * 128, 128), 128)]
+
     def hid_copy(k):
-        return remote(hgt.at[:, mine], hgt.at[:, mine], hid_s.at[k], hid_r.at[k],
-                      group_peer((group + k) % 8))
-
-    each(8, lambda k: hid_copy(k).start())
-
-    headp[...] = jnp.zeros_like(headp)
-    headp[:, 0:100] = head[...]
-    headt[...] = headp[...].T
+        return remote(hid_columns(group), hid_columns(group), hid_s.at[k], hid_r.at[k],
+                      group_peer((group + 2 * k) % 8))
+
+    def hid_wait(k):
+        return remote(hid_columns(group), hid_columns((group + 8 - 2 * k) % 8), hid_s.at[k],
+                      hid_r.at[k], group_peer((group + 2 * k) % 8))
+
+    def sib_copy(k):
+        block = hid_columns((group + 8 - 2 * k) % 8)
+        return remote(block, block, sib_s.at[k], sib_r.at[k], sibling)
+
+    def sib_wait(k):
+        block = hid_columns((sib_group + 8 - 2 * k) % 8)
+        return remote(block, block, sib_s.at[k], sib_r.at[k], sibling)
+
+    each(4, lambda k: hid_copy(k).start())
+    pending.append((4, hid_copy))
+    sib_copy(0).start()
+    pending.append((1, sib_copy))
+
+    headt[...] = jnp.zeros_like(headt)
+    headt[0:100, :] = head[...]
+    headp[...] = headt[...].T
     initp[...] = jnp.zeros_like(initp)
     initp[0:100, :] = init[...]
     truthp[...] = jnp.zeros_like(truthp)
     truthp[0:100, :] = truth[...]
-    lrow[1:2, :] = jnp.zeros_like(lrow[1:2, :])
-    diag = jnp.where(row_of == lane_of, cw[...], 0.0)
+    wts[...] = jnp.zeros_like(wts)
+    wts[0:1, 0:100] = cw[...]
+    diag = jnp.where(row_of == lane_of, wts[0:1, 0:128], 0.0)
     wts[...] = jnp.sum(diag, axis=1, keepdims=True) * lat[...]
     point_row = lax.broadcasted_iota(jnp.int32, (128, 256), 0)
     edge = (point_row == src[0:1, :]) | (point_row == src[1:2, :]) | (point_row == src[2:3, :])
@@ -163,6 +189,10 @@
 
     lax.fori_loop(0, 8, forward, 0)
 
+    each(4, lambda k: hid_wait(k).wait_recv())
+    each(4, lambda k: sib_copy(k).start())
+    pending.append((4, sib_copy))
+
     for m in range(2):
         merged = um[m, 0:1024, :]
         for i in range(4):
@@ -177,6 +207,7 @@
                       fc_s.at[k], fc_r.at[k], member_peer(to))
 
     each(8, lambda k: fc_copy(k).start())
+    pending.append((8, fc_copy))
     my_rows = pl.ds(pl.multiple_of(mem * 16, 16), 16)
     for m in range(2):
         fg[2 * mem + m] = f3[m, my_rows, :]
@@ -205,6 +236,7 @@
                       member_peer(to))
 
     each(8, lambda k: lg_copy(k).start())
+    pending.append((8, lg_copy))
     for m in range(2):
         l4[m, mem] = lloc[2 * mem + m]
     each(8, lambda k: remote(lloc.at[pl.ds(2 * mem, 2)], l4.at[:, (mem + 8 - k) % 8],
@@ -241,20 +273,18 @@
     back_above = remote(nsend.at[1], nrecv.at[:, :, 0], nh_s.at[1], nh_r.at[1], above)
     back_below.start()
     back_above.start()
+    pending.append((1, lambda k: back_below))
+    pending.append((1, lambda k: back_above))
 
     for a in range(2):
         for i in range(4):
             rows = slice(1024 * a + 256 * i, 1024 * a + 256 * i + 256)
             both = mm(um[0, rows, :], l4[0].reshape(128, 256), NT) + mm(
                 um[1, rows, :], l4[1].reshape(128, 256), NT)
-            ah[a, i] = both.astype(BF).reshape(16, 16, 128)
-
-    def ah_copy(k):
-        to = (plane + k) % 16
-        return remote(ah.at[:, :, to], ahr.at[plane], ah_s.at[k], ah_r.at[k], plane_peer(to))
-
-    each(16, lambda k: ah_copy(k).start())
-    ahr[plane] = ah[:, :, plane]
+            ah[i % 2, a, i // 2] = both.astype(BF)
+    swap = remote(ah.at[1 - core], ahx, ax_s.at[0], ax_r.at[0], sibling)
+    swap.start()
+    pending.append((1, lambda k: swap))
 
     back_below.wait_recv()
     back_above.wait_recv()
@@ -269,14 +299,31 @@
         return remote(nsnd.at[to], nrcv.at[group], na_s.at[k], na_r.at[k], group_peer(to))
 
     each(8, lambda k: na_copy(k).start())
+    pending.append((8, na_copy))
     nrcv[group] = nsnd[group]
+
+    swap.wait_recv()
+    for a in range(2):
+        for i in range(2):
+            both = ah[core, a, i].astype(F32) + ahx[a, i].astype(F32)
+            ahs[a, i] = both.astype(BF).reshape(16, 16, 128)
+
+    def ah_copy(k):
+        to = (plane + k) % 16
+        return remote(ahs.at[:, :, to], ahr.at[plane], ah_s.at[k], ah_r.at[k], plane_peer(to))
+
+    each(16, lambda k: ah_copy(k).start())
+    pending.append((16, ah_copy))
+    ahr[plane] = ahs[:, :, plane]
 
     for i in range(4):
         rows = slice(256 * i, 256 * i + 256)
-        hg_out[:, rows] = mm(nt[...], kvw[rows, :], NT)
-
-    each(8, lambda k: remote(hgt.at[:, mine], hgt.at[:, pl.ds(pl.multiple_of(((group + 8 - k) % 8) * 128, 128), 128)],
-                             hid_s.at[k], hid_r.at[k], group_peer((group + k) % 8)).wait_recv())
+        hg[:, rows] = mm(nt[...], kvw[rows, :], NT)
+    hg_copy = pltpu.make_async_copy(hg, hg_hbm, out_sem.at[0])
+    hg_copy.start()
+
+    sib_wait(0).wait_recv()
+    each(4, lambda k: sib_wait(k).wait_recv())
     each(8, lambda k: remote(nsnd.at[group], nrcv.at[(group + 8 - k) % 8], na_s.at[k], na_r.at[k],
                              group_peer((group + k) % 8)).wait_recv())
     cols256 = nrcv[...].reshape(1024, 256)
@@ -289,13 +336,19 @@
         return remote(kvp.at[:, to], kvr.at[plane], rs_s.at[k], rs_r.at[k], plane_peer(to))
 
     each(16, lambda k: rs_copy(k).start())
+    pending.append((16, rs_copy))
     kvr[plane] = kvp[:, plane]
 
-    each(16, lambda k: remote(ah.at[:, :, plane], ahr.at[(plane + 16 - k) % 16], ah_s.at[k], ah_r.at[k],
+    each(16, lambda k: remote(ahs.at[:, :, plane], ahr.at[(plane + 16 - k) % 16], ah_s.at[k], ah_r.at[k],
                               plane_peer((plane + k) % 16)).wait_recv())
     ah_sum = jnp.sum(ahr[...].astype(F32), axis=0)
-    fsnd[:, 8:16, 0:128] = ah_sum[0].reshape(8, 8, 128)
-    fsnd[:, 8:16, 128:256] = ah_sum[1].reshape(8, 8, 128)
+    for i in range(2):
+        for c in range(2):
+            at = (2 * i + core) * 2 + c
+            fsnd[at, 8:16, 0:128] = ah_sum[0, i, 8 * c:8 * c + 8]
+            fsnd[at, 8:16, 128:256] = ah_sum[1, i, 8 * c:8 * c + 8]
+            other = (2 * i + 1 - core) * 2 + c
+            fsnd[other, 8:16, :] = jnp.zeros((8, 256), F32)
     each(16, lambda k: remote(kvp.at[:, plane], kvr.at[(plane + 16 - k) % 16], rs_s.at[k], rs_r.at[k],
                               plane_peer((plane + k) % 16)).wait_recv())
     fsnd[:, 0:8, :] = jnp.sum(kvr[...].astype(F32), axis=0).reshape(8, 8, 256)
@@ -305,9 +358,22 @@
         return remote(fsnd.at[to], frcv.at[group], fin_s.at[k], fin_r.at[k], group_peer(to))
 
     each(8, lambda k: fin_copy(k).start())
+    pending.append((8, fin_copy))
     frcv[group] = fsnd[group]
     each(8, lambda k: remote(fsnd.at[group], frcv.at[(group + 8 - k) % 8], fin_s.at[k], fin_r.at[k],
                              group_peer((group + k) % 8)).wait_recv())
+    hg_copy.wait()
+
+    for count, copy in pending:
+        if count == 1:
+            copy(0).wait_send()
+        else:
+            each(count, lambda k, copy=copy: copy(k).wait_send())
+
+
+def finish(hg, frcv, headt, hg_out, kv_out, og_out, hd_out, sem):
+    copy = pltpu.make_async_copy(hg, hg_out, sem)
+    copy.start()
     for j in range(8):
         kv_out[:, 256 * j:256 * j + 256] = frcv[j, 0:8, :] * (1.0 / DEVICES)
     sums = jnp.sum(frcv[:, 8:16, :], axis=0) * (1.0 / DEVICES)
@@ -316,14 +382,7 @@
     big = outer.astype(BF)
     small = (outer - big.astype(F32)).astype(BF)
     og_out[...] = mm(big, headt[...]) + mm(small, headt[...])
-
-    to_below.wait_send()
-    to_above.wait_send()
-    back_below.wait_send()
-    back_above.wait_send()
-    for count, copy in ((8, hid_copy), (8, fc_copy), (8, lg_copy), (8, na_copy), (8, fin_copy),
-                        (16, ah_copy), (16, rs_copy)):
-        each(count, lambda k, copy=copy: copy(k).wait_send())
+    copy.wait()
 
 
 def shards(hidden, queries, kv_weight, out_weight, head_projection, initial_state, truth,
@@ -333,31 +392,40 @@
     dma = pltpu.SemaphoreType.DMA
     scratch = [
         ((2, 4, 32, 1024), BF), ((8, 256, 128), BF), ((1024, 2048), BF), ((1024, 1024), BF),
-        ((1024, 1024), BF), ((1024, 256), BF), ((1024, 128), BF), ((128, 1024), BF),
+        ((1024, 1024), BF), ((1024, 256), BF), ((1024, 128), BF),
         ((1024, 1024), BF), ((2, 2, 32, 1024), BF), ((8, 128), jnp.int32), ((16, 256, 128), BF),
         ((256, 256), F32), ((2, 8, 256, 256), BF), ((2, 8, 256, 256), F32), ((2, 2048, 256), BF),
         ((128, 256), F32), ((128, 256), F32), ((128, 256), F32), ((2, 128, 256), F32),
         ((16, 16, 256), F32), ((16, 16, 256), BF), ((2, 8, 16, 256), BF), ((2, 1024, 256), BF),
-        ((2, 1024, 256), BF), ((2, 4, 16, 16, 128), BF), ((16, 2, 4, 16, 128), BF),
+        ((2, 1024, 256), BF), ((2, 2, 2, 256, 128), BF), ((2, 2, 256, 128), BF),
+        ((2, 2, 16, 16, 128), BF), ((16, 2, 2, 16, 128), BF),
         ((16, 128, 128), F32), ((2, 16, 2, 32, 128), BF), ((16, 2, 2, 32, 128), BF),
         ((8, 128, 256), BF), ((8, 128, 256), BF), ((128, 2048), BF), ((4, 16, 16, 256), BF),
-        ((16, 4, 16, 256), BF), ((8, 16, 256), F32), ((8, 16, 256), F32),
+        ((16, 4, 16, 256), BF), ((8, 16, 256), F32), ((128, 1024), F32),
     ]
-    sems = [11, 2, 2, 8, 8, 8, 8, 8, 8, 16, 16, 2, 2, 8, 8, 16, 16, 8, 8]
-    hidden_grad, kv_grad, out_grad, head_grad = pl.pallas_call(
+    sems = [11, 1, 2, 2, 4, 4, 4, 4, 8, 8, 8, 8, 16, 16, 2, 2, 8, 8, 16, 16, 8, 8, 1, 1]
+    raw_hidden, raw_sums, head_rows = pl.pallas_call(
         body,
-        out_shape=[jax.ShapeDtypeStruct((128, 1024), F32), jax.ShapeDtypeStruct((8, 2048), F32),
-                   jax.ShapeDtypeStruct((8, 1024), F32), jax.ShapeDtypeStruct((8, 100), F32)],
+        out_shape=[jax.ShapeDtypeStruct((128, 1024), F32), jax.ShapeDtypeStruct((8, 16, 256), F32),
+                   jax.ShapeDtypeStruct((128, 1024), BF)],
         in_specs=[hbm] * 4 + [vmem] * 7,
-        out_specs=[vmem] * 4,
+        out_specs=[hbm, vmem, vmem],
         scratch_shapes=[pltpu.VMEM(shape, kind) for shape, kind in scratch] + [dma((n,)) for n in sems],
         compiler_params=pltpu.CompilerParams(
             collective_id=0, has_side_effects=True, vmem_limit_bytes=56 * 1024 * 1024),
     )(
-        hidden.reshape(2, 2, 32, 1024), queries, kv_weight, out_weight, head_projection,
-        initial_state, truth, latitude_weight.reshape(1, 256),
-        jnp.pad(channel_loss_weight, (0, 28)).reshape(1, 128), sources, halo_rows,
+        hidden.reshape(2, 2, 32, 1024), queries, kv_weight, out_weight, head_projection.T,
+        initial_state, truth, latitude_weight.reshape(1, 256), channel_loss_weight.reshape(1, 100),
+        sources, halo_rows,
     )
+    hidden_grad, kv_grad, out_grad, head_grad = pl.pallas_call(
+        finish,
+        out_shape=[jax.ShapeDtypeStruct((128, 1024), F32), jax.ShapeDtypeStruct((8, 2048), F32),
+                   jax.ShapeDtypeStruct((8, 1024), F32), jax.ShapeDtypeStruct((8, 100), F32)],
+        in_specs=[vmem, vmem, vmem],
+        out_specs=[hbm, vmem, vmem, vmem],
+        scratch_shapes=[dma(())],
+    )(raw_hidden, raw_sums, head_rows)
     return hidden_grad.reshape(2, 64, 1024), kv_grad, out_grad, head_grad
 
 

time: 93.6 us -> 74.8 us (0.80)
  Pallas kernels: 83.7 us -> 74 us
  local copies, waits for them, and re-layouts: 8.95 us -> 0 us
    pallas_call x1, Pallas kernels: 83.7 us -> 71.3 us  [shards(): pl.pallas_call(body, out_shape=[jax.ShapeDtypeStruct((128, 1024), F32), j...]
    unnamed x5 -> x0, local copies, waits for them, and re-layouts: 7.79 us -> none
    pallas_call x0 -> x1, Pallas kernels: none -> 2.62 us  [shards(): pl.pallas_call(finish, out_shape=[jax.ShapeDtypeStruct((128, 1024), F32),...]
    reshape x1 -> x0, local copies, waits for them, and re-layouts: 1.17 us -> none  [shards(): jnp.pad(channel_loss_weight, (0, 28)).reshape(1, 128)]
where the time goes in v2:
time: 74.8 us; the launch traced here: 74.6 us
  Pallas kernels  74 us (99%)
    pallas_call x1, Pallas kernels, shards(): pl.pallas_call(body, out_shape=[jax.ShapeDtypeStruct((128, 1024), F32), j...  71.3 us
    pallas_call x1, Pallas kernels, shards(): pl.pallas_call(finish, out_shape=[jax.ShapeDtypeStruct((128, 1024), F32),...  2.62 us

profile of v2, /device:TPU:1, one launch (start us, length us, event | category | flops | bytes accessed | tf_op | source)
XLA Modules:
  0.0 74.6 jit_solution(2765127541759198879)
XLA Ops:
  0.6 71.3 %shard_map.138 = (f32[128,1024]{1,0:T(8,128)}, f32[8,16,256]{2,1,0:T(8,128)}, bf16[128,1024]{1,0:T(8,128)(2,1)}) custom-call(bf16[2,2,32,1024]{3,2,1,0:T(8,128)(2,1)} %bitcast.5, bf16[256,1024]{1,0:T(8,128)(2,1)} %q_hbm.1, bf16[1024,2048]{1,0:T(8,128)(2,1)} %kvw_hbm.1, bf16[1024,1024]{1,0:T(8,128)(2,1)} %ow_hbm.1, bf16[100,1024]{1,0:T(8,128)(2,1)} %bitcast.6, ...), custom_call_target="tpu_custom_call" | custom-call | tf_op jit(solution)/shard_map/pallas_call | solution.py:407
  72.0 2.6 %shard_map.139 = (f32[128,1024]{1,0:T(8,128)}, f32[8,2048]{1,0:T(8,128)}, f32[8,1024]{1,0:T(8,128)}, f32[8,100]{1,0:T(8,128)}) custom-call(f32[128,1024]{1,0:T(8,128)} %get-tuple-element.11.hg, f32[8,16,256]{2,1,0:T(8,128)} %get-tuple-element.12.frcv, bf16[128,1024]{1,0:T(8,128)(2,1)} %get-tuple-element.13.headt), custom_call_target="tpu_custom_call" | custom-call | tf_op jit(solution)/shard_map/pallas_call | solution.py:421

commit v3 on v2

v3 whole, which is shorter than its diff:
```python
import jax
import jax.numpy as jnp
from jax import lax
from jax.experimental import pallas as pl
from jax.experimental.pallas import tpu as pltpu
from jax.sharding import PartitionSpec as P

MESH = pl.DeviceIdType.MESH
BF = jnp.bfloat16
F32 = jnp.float32
ALPHA = 0.95
SOFTENING = 0.5
MEMBERS = 16
DEVICES = 128
NN = (((1,), (0,)), ((), ()))
NT = (((1,), (1,)), ((), ()))


def mm(a, b, dims=NN):
    return lax.dot_general(a, b, dims, preferred_element_type=F32)


def rem(a, n):
    return lax.rem(a, jnp.int32(n))


def div(a, n):
    return lax.div(a, jnp.int32(n))


def body(
    hid_hbm, q_hbm, kvw_hbm, ow_hbm, head, init, truth, lat, cw, src, halo,
    hg_hbm, frcv,
    ext, q3, kvw, ow, owt, qt, headp, headt, hgt, pick, lrow, kv3, mask, gt, dsg, um,
    initp, truthp, wts, f3, fg, lloc, l4, ug, dm, ah, ahx, ahs, ahr, nown, nsend, nrecv, nt, nsnd,
    nrcv, kvp, kvr, fsnd, hg,
    in_sem, out_sem, halo_s, halo_r, hid_s, hid_r, sib_s, sib_r, fc_s, fc_r, lg_s, lg_r,
    ah_s, ah_r, nh_s, nh_r, na_s, na_r, rs_s, rs_r, fin_s, fin_r, ax_s, ax_r,
):
    mem, band = lax.axis_index("member"), lax.axis_index("band")
    z, ylo = div(mem, 2), rem(mem, 2)
    core = rem(band, 2)
    group = z * 2 + core
    plane = ylo * 8 + div(band, 2)
    sibling = (mem, band + 1 - 2 * core)
    below, above = (mem, rem(band + 15, 16)), (mem, rem(band + 1, 16))
    pending = []

    def group_peer(j):
        return div(j, 2) * 2 + ylo, band - core + rem(j, 2)

    def plane_peer(q):
        return z * 2 + div(q, 8), rem(q, 8) * 2 + core

    def member_peer(m):
        return m, band

    def remote(source, target, send, recv, device):
        return pltpu.make_async_remote_copy(
            src_ref=source, dst_ref=target, send_sem=send, recv_sem=recv,
            device_id=device, device_id_type=MESH)

    def sent(bulk, send, recv):
        pending.append(remote(bulk, bulk, send, recv, sibling))

    def received(bulk, send, recv):
        remote(bulk, bulk, send, recv, sibling).wait_recv()

    def flush():
        while pending:
            pending.pop(0).wait_send()

    loads = [pltpu.make_async_copy(hid_hbm, ext.at[:, 0:2], in_sem.at[0]),
             pltpu.make_async_copy(kvw_hbm, kvw, in_sem.at[1]),
             pltpu.make_async_copy(ow_hbm, ow, in_sem.at[2])]
    loads += [pltpu.make_async_copy(q_hbm.at[:, 128 * p:128 * p + 128], q3.at[p], in_sem.at[3 + p])
              for p in range(8)]
    for copy in loads:
        copy.start()

    barrier = pltpu.get_barrier_semaphore()

    def greet(device):
        pl.semaphore_signal(barrier, inc=1, device_id=device, device_id_type=MESH)

    greet(below)
    greet(above)
    for k in range(1, 8):
        greet(group_peer(rem(group + k, 8)))
    for k in range(4):
        greet(member_peer(rem(mem + 2 * k + 1, 8)))
    for k in range(1, 16):
        greet(plane_peer(rem(plane + k, 16)))

    for m in range(2):
        for d in range(2):
            at = 64 * m + 32 * d
            lrow[0:1, at:at + 32] = halo[d:d + 1, :] + 64 * m
    row_of = lax.broadcasted_iota(jnp.int32, (128, 128), 0)
    lane_of = lax.broadcasted_iota(jnp.int32, (128, 128), 1)
    scatter = (row_of == lrow[0:1, :]).astype(F32)
    gather = scatter.T.astype(BF)
    scatter = scatter.astype(BF)

    loads[0].wait()
    own = ext[:, 0:2].reshape(128, 1024)
    for n in range(4):
        cols = slice(256 * n, 256 * n + 256)
        pick[:, :, :, cols] = mm(gather, own[:, cols]).astype(BF).reshape(2, 2, 32, 256)

    pl.semaphore_wait(barrier, 28)
    to_below = remote(pick.at[:, 0], ext.at[:, 3], halo_s.at[0], halo_r.at[0], below)
    to_above = remote(pick.at[:, 1], ext.at[:, 2], halo_s.at[1], halo_r.at[1], above)
    to_below.start()
    to_above.start()
    pending.extend([to_below, to_above])

    mine = pl.ds(pl.multiple_of(group * 128, 128), 128)
    for n in range(8):
        rows = slice(128 * n, 128 * n + 128)
        hgt[rows, mine] = own[:, rows].T

    def hid_columns(j):
        return hgt.at[:, pl.ds(pl.multiple_of(j * 128, 128), 128)]

    for k in (2, 1, 3):
        remote(hid_columns(group), hid_columns(group), hid_s, hid_r,
               group_peer(rem(group + 2 * k, 8))).start()
    remote(hid_columns(group), hid_columns(group), sib_s, sib_r, sibling).start()

    headt[...] = jnp.zeros_like(headt)
    headt[0:100, :] = head[...]
    headp[...] = headt[...].T
    initp[...] = jnp.zeros_like(initp)
    initp[0:100, :] = init[...]
    truthp[...] = jnp.zeros_like(truthp)
    truthp[0:100, :] = truth[...]
    wts[...] = jnp.zeros_like(wts)
    wts[0:1, 0:100] = cw[...]
    diag = jnp.where(row_of == lane_of, wts[0:1, 0:128], 0.0)
    wts[...] = jnp.sum(diag, axis=1, keepdims=True) * lat[...]
    point_row = lax.broadcasted_iota(jnp.int32, (128, 256), 0)
    edge = (point_row == src[0:1, :]) | (point_row == src[1:2, :]) | (point_row == src[2:3, :])
    mask[0:128, :] = edge.astype(F32)
    mask[128:256, :] = edge.astype(F32)
    lo_lane = (lane_of < 64).astype(BF)
    hi_lane = (lane_of >= 64).astype(BF)
    lo_row = (row_of < 64).astype(BF)
    hi_row = (row_of >= 64).astype(BF)
    for p in range(8):
        loads[3 + p].wait()
        qt[128 * p:128 * p + 128, :] = q3[p].T
    loads[2].wait()
    for i in range(4):
        rows = slice(256 * i, 256 * i + 256)
        for j in range(4):
            cols = slice(256 * j, 256 * j + 256)
            owt[rows, cols] = ow[cols, rows].T

    loads[1].wait()
    to_below.wait_recv()
    to_above.wait_recv()
    rows256 = ext[...].reshape(256, 1024)
    for n in range(8):
        part = mm(rows256, kvw[:, 256 * n:256 * n + 256]).astype(BF)
        kv3[2 * n] = part[:, :128]
        kv3[2 * n + 1] = part[:, 128:]

    my_rows = pl.ds(pl.multiple_of(mem * 16, 16), 16)
    for m in range(2):
        for p in range(8):
            kp = kv3[p, 128 * m:128 * m + 128, :]
            vt = kv3[8 + p, 128 * m:128 * m + 128, :].T
            kcat = jnp.concatenate([kp * lo_lane, kp * hi_lane], axis=0)
            score = mm(kcat, q3[p], NT)
            th = jnp.tanh(score * (0.5 / 8.0))
            on = mask[...]
            gate = ((0.5 + 0.5 * th) * on).astype(BF)
            gt[m, p] = gate
            dsg[m, p] = (0.25 - 0.25 * th * th) * (on * 0.125)
            vcat_t = jnp.concatenate([vt * lo_row, vt * hi_row], axis=1)
            um[m, 128 * p:128 * p + 128, :] = mm(vcat_t, gate).astype(BF)
        merged = um[m, 0:1024, :]
        for i in range(4):
            rows = slice(256 * i, 256 * i + 256)
            up = mm(owt[rows, :], merged) + qt[rows, :].astype(F32)
            um[m, 1024 + 256 * i:1024 + 256 * i + 256, :] = up.astype(BF)
        f3[m] = mm(headt[...], um[m, 1024:2048, :]) + initp[...]
        for k in range(7, 0, -1):
            to = rem(mem + k, 8)
            remote(f3.at[m, pl.ds(pl.multiple_of(to * 16, 16), 16), :], fg.at[2 * mem + m],
                   fc_s.at[m], fc_r.at[m], member_peer(to)).start()
        sent(fg.at[0:7], fc_s.at[m], fc_r.at[m])
        fg[2 * mem + m] = f3[m, my_rows, :]

    sent(hgt.at[:, 0:384], hid_s, hid_r)
    received(hgt.at[:, 0:384], hid_s, hid_r)
    for k in (1, 2, 3):
        block = hid_columns(rem(group + 2 * k, 8))
        remote(block, block, sib_s, sib_r, sibling).start()
    sent(hgt.at[:, 0:512], sib_s, sib_r)
    for m in range(2):
        received(fg.at[0:7], fc_s.at[m], fc_r.at[m])

    spread = (1.0 - (1.0 - ALPHA) / MEMBERS) / (MEMBERS * (MEMBERS - 1))
    soft = SOFTENING * SOFTENING
    truth_rows = truthp[my_rows, :]
    weight = wts[my_rows, :]

    for k in (4, 3, 5, 2, 6, 1, 7, 0):
        to = rem(mem + k, 8)
        for i in range(2):
            f = fg[2 * to + i]
            gap = f[None] - fg[...]
            slopes = jnp.sum(gap * lax.rsqrt(gap * gap + soft), axis=0)
            off = f - truth_rows
            slope = off * lax.rsqrt(off * off + soft)
            lloc[2 * to + i] = (weight * (slope * (1.0 / MEMBERS) - spread * slopes)).astype(BF)
        if k:
            remote(lloc.at[pl.ds(2 * to, 2)], l4.at[:, mem], lg_s, lg_r, member_peer(to)).start()
    sent(lloc.at[0:14], lg_s, lg_r)
    for m in range(2):
        l4[m, mem] = lloc[2 * mem + m]
    received(lloc.at[0:14], lg_s, lg_r)

    for m in range(2):
        grad = l4[m].reshape(128, 256)
        for i in range(4):
            rows = slice(256 * i, 256 * i + 256)
            ug[m, rows, :] = mm(headp[rows, :], grad).astype(BF)
    low = lane_of < 64
    order = (2, 1, 3, 0)

    def back_copy(h, step, d, inward=False):
        g = rem(z + order[step], 4)
        side = d if inward else 1 - d
        return remote(nsend.at[d, h, g], nrecv.at[h, g, :, side], nh_s.at[h, step, d],
                      nh_r.at[h, step, side], (below, above)[d])

    def keep(h, g, i, m, both):
        cols = slice(128 * i, 128 * i + 128)
        rows = jnp.where(low, both[:128], both[128:])
        nown[h, g, 64 * m:64 * m + 64, cols] = rows[0:64]
        nsend[0, h, g, m, :, cols] = rows[64:96].astype(BF)
        nsend[1, h, g, m, :, cols] = rows[96:128].astype(BF)

    def send_back(h, step):
        for d in range(2):
            copy = back_copy(h, step, d)
            copy.start()
            pending.append(copy)

    for step in range(4):
        g = rem(z + order[step], 4)
        rows = pl.ds(pl.multiple_of(g * 256, 256), 256)
        for m in range(2):
            dm[m, rows, :] = mm(ow[rows, :], ug[m]).astype(BF)
        for i in range(2):
            p = 2 * g + i
            for m in range(2):
                grad = dm[m, pl.ds(pl.multiple_of(p * 128, 128), 128), :]
                keep(0, g, i, m, mm(gt[m, p], grad, NT))
        send_back(0, step)
    for step in range(4):
        g = rem(z + order[step], 4)
        for i in range(2):
            p = 2 * g + i
            for m in range(2):
                vp = kv3[8 + p, 128 * m:128 * m + 128, :]
                vcat = jnp.concatenate([vp * lo_lane, vp * hi_lane], axis=0)
                grad = dm[m, pl.ds(pl.multiple_of(p * 128, 128), 128), :]
                score_grad = (mm(vcat, grad) * dsg[m, p]).astype(BF)
                keep(1, g, i, m, mm(score_grad, q3[p]))
        send_back(1, step)

    def node_step(h, step):
        g = rem(z + order[step], 4)
        for d in range(2):
            back_copy(h, step, d, True).wait_recv()
        total = (nown[h, g] + mm(scatter, nrecv[h, g].reshape(128, 256))).astype(BF)
        nt[:, pl.ds(pl.multiple_of(1024 * (1 - h) + g * 256, 256), 256)] = total
        for c in range(2):
            nsnd[h, 2 * g + c] = total[:, 128 * c:128 * c + 128]
        if step < 3:
            for c in range(2):
                remote(nsnd.at[h, 2 * g + c], nrcv.at[h, group], na_s.at[h], na_r.at[h],
                       group_peer(2 * g + c)).start()
        else:
            remote(nsnd.at[h, group + 1 - 2 * core], nrcv.at[h, group], na_s.at[h], na_r.at[h],
                   sibling).start()
            sent(nrcv.at[h, 0:7], na_s.at[h], na_r.at[h])
            nrcv[h, group] = nsnd[h, group]

    for step in range(4):
        node_step(0, step)

    for a in range(2):
        for i in range(4):
            rows = slice(1024 * a + 256 * i, 1024 * a + 256 * i + 256)
            both = mm(um[0, rows, :], l4[0].reshape(128, 256), NT) + mm(
                um[1, rows, :], l4[1].reshape(128, 256), NT)
            ah[i % 2, a, i // 2] = both.astype(BF)
    swap = remote(ah.at[1 - core], ahx, ax_s, ax_r, sibling)
    swap.start()
    pending.append(swap)

    for step in range(4):
        node_step(1, step)

    swap.wait_recv()
    for a in range(2):
        for i in range(2):
            both = ah[core, a, i].astype(F32) + ahx[a, i].astype(F32)
            ahs[a, i] = both.astype(BF).reshape(16, 16, 128)
    for k in range(1, 16):
        to = rem(plane + k, 16)
        remote(ahs.at[:, :, to], ahr.at[plane], ah_s, ah_r, plane_peer(to)).start()
    sent(ahr.at[0:15], ah_s, ah_r)
    ahr[plane] = ahs[:, :, plane]

    received(hgt.at[:, 0:512], sib_s, sib_r)
    for h in range(2):
        received(nrcv.at[h, 0:7], na_s.at[h], na_r.at[h])
        node_cols = nrcv[h].reshape(1024, 128)
        for i in range(4):
            rows = slice(256 * i, 256 * i + 256)
            kvp[h, i] = mm(hgt[rows, :], node_cols).astype(BF).reshape(16, 16, 128)
        for k in range(1, 16):
            to = rem(plane + k, 16)
            remote(kvp.at[h, :, to], kvr.at[h, plane], rs_s.at[h], rs_r.at[h], plane_peer(to)).start()
        kvr[h, plane] = kvp[h, :, plane]

    for i in range(4):
        rows = slice(256 * i, 256 * i + 256)
        hg[:, rows] = mm(nt[...], kvw[rows, :], NT)
    hg_copy = pltpu.make_async_copy(hg, hg_hbm, out_sem)
    hg_copy.start()
    flush()

    received(ahr.at[0:15], ah_s, ah_r)
    ah_sum = jnp.sum(ahr[...].astype(F32), axis=0)
    for i in range(2):
        for c in range(2):
            at = (2 * i + core) * 2 + c
            fsnd[at, 8:16, 0:128] = ah_sum[0, i, 8 * c:8 * c + 8]
            fsnd[at, 8:16, 128:256] = ah_sum[1, i, 8 * c:8 * c + 8]
            other = (2 * i + 1 - core) * 2 + c
            fsnd[other, 8:16, :] = jnp.zeros((8, 256), F32)
    for h in range(2):
        received(kvr.at[h, 0:15], rs_s.at[h], rs_r.at[h])
        kv_sum = jnp.sum(kvr[h].astype(F32), axis=0)
        fsnd[:, 0:8, 128 * h:128 * h + 128] = kv_sum.reshape(8, 8, 128)
    for k in (4, 5, 2, 3, 6, 7, 1):
        to = rem(group + k, 8)
        remote(fsnd.at[to], frcv.at[group], fin_s, fin_r, group_peer(to)).start()
    frcv[group] = fsnd[group]
    for h in range(2):
        sent(kvr.at[h, 0:15], rs_s.at[h], rs_r.at[h])
    sent(fsnd.at[0:7], fin_s, fin_r)
    flush()
    hg_copy.wait()
    received(frcv.at[0:7], fin_s, fin_r)


def finish(hg, frcv, head, hg_out, kv_out, og_out, hd_out, headt, sem):
    copy = pltpu.make_async_copy(hg, hg_out, sem)
    copy.start()
    headt[...] = jnp.zeros_like(headt)
    headt[0:100, :] = head[...]
    for j in range(8):
        at = 128 * j
        kv_out[:, at:at + 128] = frcv[j, 0:8, 128:256] * (1.0 / DEVICES)
        kv_out[:, 1024 + at:1024 + at + 128] = frcv[j, 0:8, 0:128] * (1.0 / DEVICES)
    sums = jnp.sum(frcv[:, 8:16, :], axis=0) * (1.0 / DEVICES)
    hd_out[...] = sums[:, 128:228]
    outer = sums[:, 0:128]
    big = outer.astype(BF)
    small = (outer - big.astype(F32)).astype(BF)
    og_out[...] = mm(big, headt[...]) + mm(small, headt[...])
    copy.wait()


def shards(hidden, queries, kv_weight, out_weight, head_projection, initial_state, truth,
           latitude_weight, channel_loss_weight, sources, halo_rows):
    vmem = pl.BlockSpec(memory_space=pltpu.VMEM)
    hbm = pl.BlockSpec(memory_space=pl.ANY)
    dma = pltpu.SemaphoreType.DMA
    scratch = [
        ((2, 4, 32, 1024), BF), ((8, 256, 128), BF), ((1024, 2048), BF), ((1024, 1024), BF),
        ((1024, 1024), BF), ((1024, 256), BF), ((1024, 128), BF), ((128, 1024), BF),
        ((1024, 1024), BF), ((2, 2, 32, 1024), BF), ((8, 128), jnp.int32), ((16, 256, 128), BF),
        ((256, 256), F32), ((2, 8, 256, 256), BF), ((2, 8, 256, 256), F32), ((2, 2048, 256), BF),
        ((128, 256), F32), ((128, 256), F32), ((128, 256), F32), ((2, 128, 256), F32),
        ((16, 16, 256), F32), ((16, 16, 256), BF), ((2, 8, 16, 256), BF), ((2, 1024, 256), BF),
        ((2, 1024, 256), BF), ((2, 2, 2, 256, 128), BF), ((2, 2, 256, 128), BF),
        ((2, 2, 16, 16, 128), BF), ((16, 2, 2, 16, 128), BF),
        ((2, 4, 128, 256), F32), ((2, 2, 4, 2, 32, 256), BF), ((2, 4, 2, 2, 32, 256), BF),
        ((128, 2048), BF), ((2, 8, 128, 128), BF), ((2, 8, 128, 128), BF),
        ((2, 4, 16, 16, 128), BF), ((2, 16, 4, 16, 128), BF), ((8, 16, 256), F32),
        ((128, 1024), F32),
    ]
    sems = [(11,), (), (2,), (2,), (), (), (), (), (2,), (2,), (), (), (), (), (2, 4, 2), (2, 4, 2),
            (2,), (2,), (2,), (2,), (), (), (), ()]
    raw_hidden, raw_sums = pl.pallas_call(
        body,
        out_shape=[jax.ShapeDtypeStruct((128, 1024), F32), jax.ShapeDtypeStruct((8, 16, 256), F32)],
        in_specs=[hbm] * 4 + [vmem] * 7,
        out_specs=[hbm, vmem],
        scratch_shapes=[pltpu.VMEM(shape, kind) for shape, kind in scratch] + [dma(n) for n in sems],
        compiler_params=pltpu.CompilerParams(
            collective_id=0, has_side_effects=True, vmem_limit_bytes=56 * 1024 * 1024),
    )(
        hidden.reshape(2, 2, 32, 1024), queries, kv_weight, out_weight, head_projection.T,
        initial_state, truth, latitude_weight.reshape(1, 256), channel_loss_weight.reshape(1, 100),
        sources, halo_rows,
    )
    hidden_grad, kv_grad, out_grad, head_grad = pl.pallas_call(
        finish,
        out_shape=[jax.ShapeDtypeStruct((128, 1024), F32), jax.ShapeDtypeStruct((8, 2048), F32),
                   jax.ShapeDtypeStruct((8, 1024), F32), jax.ShapeDtypeStruct((8, 100), F32)],
        in_specs=[vmem, vmem, vmem],
        out_specs=[hbm, vmem, vmem, vmem],
        scratch_shapes=[pltpu.VMEM((128, 1024), BF), dma(())],
    )(raw_hidden, raw_sums, head_projection.T)
    return hidden_grad.reshape(2, 64, 1024), kv_grad, out_grad, head_grad


def solution(mesh):
    placed = (
        P("member", "band", None),
        P("band", None),
        P(),
        P(),
        P(),
        P(None, "band"),
        P(None, "band"),
        P("band"),
        P(),
        P(None, "band"),
        P("band", None),
    )
    return jax.shard_map(
        shards,
        mesh=mesh,
        in_specs=placed,
        out_specs=(
            P("member", "band", None),
            P(("member", "band"), None),
            P(("member", "band"), None),
            P(("member", "band"), None),
        ),
        check_vma=False,
    )
```

time: 74.8 us -> 60.9 us (0.81)
  Pallas kernels: 74 us -> 60 us
    pallas_call x1, Pallas kernels: 71.3 us -> 57.4 us  [shards(): pl.pallas_call(body, out_shape=[jax.ShapeDtypeStruct((128, 1024), F32), j...]
where the time goes in v3:
time: 60.9 us; the launch traced here: 60.8 us
  Pallas kernels  60 us (99%)
  between operations  0.8 us (1%)
    pallas_call x1, Pallas kernels, shards(): pl.pallas_call(body, out_shape=[jax.ShapeDtypeStruct((128, 1024), F32), j...  57.4 us
    pallas_call x1, Pallas kernels, shards(): pl.pallas_call(finish, out_shape=[jax.ShapeDtypeStruct((128, 1024), F32),...  2.6 us

profile of v3, /device:TPU:1, one launch (start us, length us, event | category | flops | bytes accessed | tf_op | source)
XLA Modules:
  0.0 60.8 jit_solution(9601060102842752919)
XLA Ops:
  0.6 57.4 %shard_map.138 = (f32[128,1024]{1,0:T(8,128)}, f32[8,16,256]{2,1,0:T(8,128)}) custom-call(bf16[2,2,32,1024]{3,2,1,0:T(8,128)(2,1)} %bitcast.7, bf16[256,1024]{1,0:T(8,128)(2,1)} %q_hbm.1, bf16[1024,2048]{1,0:T(8,128)(2,1)} %kvw_hbm.1, bf16[1024,1024]{1,0:T(8,128)(2,1)} %ow_hbm.1, bf16[100,1024]{1,0:T(8,128)(2,1)} %bitcast.5, f32[100,256]{1,0:T(8,128)} %init.1, ...), custom_call_target="tpu_custom_call" | custom-call | tf_op jit(solution)/shard_map/pallas_call | solution.py:404
  58.0 2.6 %shard_map.139 = (f32[128,1024]{1,0:T(8,128)}, f32[8,2048]{1,0:T(8,128)}, f32[8,1024]{1,0:T(8,128)}, f32[8,100]{1,0:T(8,128)}) custom-call(f32[128,1024]{1,0:T(8,128)} %get-tuple-element.10.hg, f32[8,16,256]{2,1,0:T(8,128)} %get-tuple-element.11.frcv, bf16[100,1024]{1,0:T(8,128)(2,1)} %bitcast.6), custom_call_target="tpu_custom_call" | custom-call | tf_op jit(solution)/shard_map/pallas_call | solution.py:417

commit v4 on v3

v4 whole, which is shorter than its diff:
```python
import jax
import jax.numpy as jnp
from jax import lax
from jax.experimental import pallas as pl
from jax.experimental.pallas import tpu as pltpu
from jax.sharding import PartitionSpec as P

MESH = pl.DeviceIdType.MESH
BF = jnp.bfloat16
F32 = jnp.float32
ALPHA = 0.95
SOFTENING = 0.5
MEMBERS = 16
DEVICES = 128
NN = (((1,), (0,)), ((), ()))
NT = (((1,), (1,)), ((), ()))


def mm(a, b, dims=NN):
    return lax.dot_general(a, b, dims, preferred_element_type=F32)


def rem(a, n):
    return lax.rem(a, jnp.int32(n))


def div(a, n):
    return lax.div(a, jnp.int32(n))


def body(
    hid_hbm, q_hbm, kvw_hbm, ow_hbm, head_hbm, init_hbm, truth_hbm, lat_hbm, cw_hbm, src_hbm, halo_hbm,
    hg_hbm, frcv,
    head, init, truth, lat, cw, src, halo,
    ext, q3, kvw, ow, owt, qt, headp, headt, hgt, pick, lrow, kvo, kvh, vto, mask, gt, dsg, um,
    initp, truthp, wts, f3, fg, lloc, l4, ug, dm, ah, ahx, ahs, ahr, ahs2, ahr2, nown, nsend, nrecv, nt, nsnd,
    nrcv, kvp, kvr, fsnd, hg,
    in_sem, out_sem, halo_s, halo_r, hid_s, hid_r, sib_s, sib_r, fc_s, fc_r, lg_s, lg_r,
    ah_s, ah_r, ay_s, ay_r, nh_s, nh_r, na_s, na_r, rs_s, rs_r, fin_s, fin_r, ax_s, ax_r,
):
    mem, band = lax.axis_index("member"), lax.axis_index("band")
    z, ylo = div(mem, 2), rem(mem, 2)
    core = rem(band, 2)
    group = z * 2 + core
    plane = ylo * 8 + div(band, 2)
    x, yhi = div(band, 4), rem(div(band, 2), 2)
    y = yhi * 2 + ylo
    sibling = (mem, band + 1 - 2 * core)
    below, above = (mem, rem(band + 15, 16)), (mem, rem(band + 1, 16))
    pending = []

    def group_peer(j):
        return div(j, 2) * 2 + ylo, band - core + rem(j, 2)

    def plane_peer(q):
        return z * 2 + div(q, 8), rem(q, 8) * 2 + core

    def member_peer(m):
        return m, band

    def remote(source, target, send, recv, device):
        return pltpu.make_async_remote_copy(
            src_ref=source, dst_ref=target, send_sem=send, recv_sem=recv,
            device_id=device, device_id_type=MESH)

    def sent(bulk, send, recv):
        pending.append(remote(bulk, bulk, send, recv, sibling))

    def received(bulk, send, recv):
        remote(bulk, bulk, send, recv, sibling).wait_recv()

    def flush():
        while pending:
            pending.pop(0).wait_send()

    loads = [pltpu.make_async_copy(source, target, in_sem.at[i]) for i, (source, target) in enumerate([
        (halo_hbm, halo), (hid_hbm, ext.at[:, 0:2]), (src_hbm, src), (lat_hbm, lat), (cw_hbm, cw),
        (init_hbm, init), (truth_hbm, truth), (head_hbm, head), (ow_hbm, ow), (kvw_hbm, kvw)])]
    loads += [pltpu.make_async_copy(q_hbm.at[:, 128 * p:128 * p + 128], q3.at[p], in_sem.at[10 + p])
              for p in range(8)]
    loads[0].start()
    loads[1].start()

    barrier = pltpu.get_barrier_semaphore()

    def greet(device):
        pl.semaphore_signal(barrier, inc=1, device_id=device, device_id_type=MESH)

    for k in (10, 9, 11, 6, 5, 7, 8, 2, 13, 14, 3, 1, 15, 4, 12):
        greet(plane_peer(rem(plane + k, 16)))
    greet(below)
    greet(above)
    for k in range(4):
        greet(member_peer(rem(mem + 2 * k + 1, 8)))
    for k in range(1, 8):
        greet(group_peer(rem(group + k, 8)))

    loads[0].wait()
    for m in range(2):
        for d in range(2):
            at = 64 * d + 32 * m
            lrow[0:1, at:at + 32] = halo[d:d + 1, :] + 64 * m
    row_of = lax.broadcasted_iota(jnp.int32, (128, 128), 0)
    lane_of = lax.broadcasted_iota(jnp.int32, (128, 128), 1)
    scatter = (row_of == lrow[0:1, :]).astype(F32)
    gather = scatter.T.astype(BF)
    scatter = scatter.astype(BF)

    loads[1].wait()
    for copy in loads[2:8] + loads[10:] + loads[8:10]:
        copy.start()
    own = ext[:, 0:2].reshape(128, 1024)
    for n in range(4):
        cols = slice(256 * n, 256 * n + 256)
        pick[:, :, :, cols] = mm(gather, own[:, cols]).astype(BF).reshape(2, 2, 32, 256)

    pl.semaphore_wait(barrier, 28)
    to_below = remote(pick.at[0], ext.at[:, 3], halo_s.at[0], halo_r.at[0], below)
    to_above = remote(pick.at[1], ext.at[:, 2], halo_s.at[1], halo_r.at[1], above)
    to_below.start()
    to_above.start()
    pending.extend([to_below, to_above])

    for n in range(8):
        rows = slice(128 * n, 128 * n + 128)
        hgt[group, rows, :] = own[:, rows].T
    pieces = (pl.ds(0, 512), pl.ds(512, 256), pl.ds(768, 256))

    def hid_piece(a, j):
        return hgt.at[j, pieces[a]]

    def hid_bulk(a):
        return hgt.at[0:3, pieces[a]]

    def hid_send(a):
        for k in (2, 1, 3):
            remote(hid_piece(a, group), hid_piece(a, group), hid_s.at[a], hid_r.at[a],
                   group_peer(rem(group + 2 * k, 8))).start()
        sent(hid_bulk(a), hid_s.at[a], hid_r.at[a])

    def hid_forward(a):
        received(hid_bulk(a), hid_s.at[a], hid_r.at[a])
        for k in (1, 2, 3):
            block = hid_piece(a, rem(group + 2 * k, 8))
            remote(block, block, sib_s.at[a], sib_r.at[a], sibling).start()
        sent(hid_bulk(a), sib_s.at[a], sib_r.at[a])

    hid_send(0)
    remote(hgt.at[group], hgt.at[group], sib_s.at[3], sib_r.at[3], sibling).start()
    sent(hgt.at[0], sib_s.at[3], sib_r.at[3])

    for copy in loads[2:8]:
        copy.wait()
    headt[...] = jnp.zeros_like(headt)
    headt[0:100, :] = head[...]
    headp[...] = headt[...].T
    initp[...] = jnp.zeros_like(initp)
    initp[0:100, :] = init[...]
    truthp[...] = jnp.zeros_like(truthp)
    truthp[0:100, :] = truth[...]
    wts[...] = jnp.zeros_like(wts)
    wts[0:1, 0:100] = cw[...]
    diag = jnp.where(row_of == lane_of, wts[0:1, 0:128], 0.0)
    wts[...] = jnp.sum(diag, axis=1, keepdims=True) * lat[...]
    point_row = lax.broadcasted_iota(jnp.int32, (128, 256), 0)
    edge = (point_row == src[0:1, :]) | (point_row == src[1:2, :]) | (point_row == src[2:3, :])
    edge = edge.astype(F32)
    for at in (0, 64):
        mask[at:at + 64, :] = edge[0:64]
        mask[128 + at:128 + at + 64, :] = edge[64:128]
    lo_lane = (lane_of < 64).astype(BF)[0:64]
    hi_lane = (lane_of >= 64).astype(BF)[0:64]
    for p in range(8):
        loads[10 + p].wait()
        qt[128 * p:128 * p + 128, :] = q3[p].T
    loads[8].wait()
    for i in range(4):
        rows = slice(256 * i, 256 * i + 256)
        for j in range(4):
            cols = slice(256 * j, 256 * j + 256)
            owt[rows, cols] = ow[cols, rows].T

    def project(rows, target):
        for n in range(8):
            part = mm(rows, kvw[:, 256 * n:256 * n + 256]).astype(BF)
            target[2 * n] = part[:, :128]
            target[2 * n + 1] = part[:, 128:]

    def by_head(block):
        return jnp.concatenate([block * lo_lane, block * hi_lane], axis=0)

    def gates(part, source, m, p):
        at = slice(128 * part, 128 * part + 128)
        score = mm(by_head(source[p, 64 * m:64 * m + 64, :]), q3[p], NT)
        th = jnp.tanh(score * (0.5 / 8.0))
        on = mask[at, :]
        gate = ((0.5 + 0.5 * th) * on).astype(BF)
        gt[m, p, at, :] = gate
        dsg[m, p, at, :] = (0.25 - 0.25 * th * th) * (on * 0.125)
        return gate

    loads[9].wait()
    project(own, kvo)
    for m in range(2):
        for p in range(8):
            gates(0, kvo, m, p)
            vto[m, p] = by_head(kvo[8 + p, 64 * m:64 * m + 64, :]).T
    to_below.wait_recv()
    to_above.wait_recv()
    project(ext[:, 2:4].reshape(128, 1024), kvh)

    my_rows = pl.ds(pl.multiple_of(mem * 16, 16), 16)
    for m in range(2):
        for p in range(8):
            gate = jnp.concatenate([gt[m, p, 0:128, :], gates(1, kvh, m, p)], axis=0)
            value = by_head(kvh[8 + p, 64 * m:64 * m + 64, :]).T
            value = jnp.concatenate([vto[m, p], value], axis=1)
            um[m, 128 * p:128 * p + 128, :] = mm(value, gate).astype(BF)
        merged = um[m, 0:1024, :]
        for i in range(4):
            rows = slice(256 * i, 256 * i + 256)
            up = mm(owt[rows, :], merged) + qt[rows, :].astype(F32)
            um[m, 1024 + 256 * i:1024 + 256 * i + 256, :] = up.astype(BF)
        f3[m] = mm(headt[...], um[m, 1024:2048, :]) + initp[...]
        for k in range(7, 0, -1):
            to = rem(mem + k, 8)
            remote(f3.at[m, pl.ds(pl.multiple_of(to * 16, 16), 16), :], fg.at[2 * mem + m],
                   fc_s.at[m], fc_r.at[m], member_peer(to)).start()
        sent(fg.at[0:7], fc_s.at[m], fc_r.at[m])
        fg[2 * mem + m] = f3[m, my_rows, :]

    hid_forward(0)
    hid_send(1)
    for m in range(2):
        received(fg.at[0:7], fc_s.at[m], fc_r.at[m])

    spread = (1.0 - (1.0 - ALPHA) / MEMBERS) / (MEMBERS * (MEMBERS - 1))
    soft = SOFTENING * SOFTENING
    truth_rows = truthp[my_rows, :]
    weight = wts[my_rows, :]

    def loss(k):
        to = rem(mem + k, 8)
        for i in range(2):
            f = fg[2 * to + i]
            gap = f[None] - fg[...]
            slopes = jnp.sum(gap * lax.rsqrt(gap * gap + soft), axis=0)
            off = f - truth_rows
            slope = off * lax.rsqrt(off * off + soft)
            lloc[2 * to + i] = (weight * (slope * (1.0 / MEMBERS) - spread * slopes)).astype(BF)

    for part in ((4, 3, 5), (2, 6, 1), (7, 0)):
        for k in part:
            loss(k)
        for k in part:
            if k:
                to = rem(mem + k, 8)
                remote(lloc.at[pl.ds(2 * to, 2)], l4.at[:, mem], lg_s, lg_r, member_peer(to)).start()
    sent(lloc.at[0:14], lg_s, lg_r)
    hid_forward(1)
    hid_send(2)
    for m in range(2):
        l4[m, mem] = lloc[2 * mem + m]
    received(lloc.at[0:14], lg_s, lg_r)

    for m in range(2):
        grad = l4[m].reshape(128, 256)
        for i in range(4):
            rows = slice(256 * i, 256 * i + 256)
            ug[m, rows, :] = mm(headp[rows, :], grad).astype(BF)
    low = (lane_of < 64)[0:64]
    order = (2, 1, 3, 0)

    def back_copy(h, step, d, inward=False):
        side = d if inward else 1 - d
        return remote(nsend.at[d, h, step], nrecv.at[h, step, side], nh_s.at[h, step, d],
                      nh_r.at[h, step, side], (below, above)[d])

    def keep(h, step, i, m, both):
        cols = slice(128 * i, 128 * i + 128)
        nown[h, step, 64 * m:64 * m + 64, cols] = jnp.where(low, both[0:64], both[64:128])
        halo_part = jnp.where(low, both[128:192], both[192:256]).astype(BF)
        nsend[0, h, step, m, :, cols] = halo_part[0:32]
        nsend[1, h, step, m, :, cols] = halo_part[32:64]

    def send_back(h, step):
        for d in range(2):
            copy = back_copy(h, step, d)
            copy.start()
            pending.append(copy)

    def merged_grad(step):
        rows = pl.ds(pl.multiple_of(rem(z + order[step], 4) * 256, 256), 256)
        for m in range(2):
            dm[step, m] = mm(ow[rows, :], ug[m]).astype(BF)

    merged_grad(0)
    for step in range(4):
        for i in range(2):
            for m in range(2):
                p = 2 * rem(z + order[step], 4) + i
                keep(0, step, i, m, mm(gt[m, p], dm[step, m, 128 * i:128 * i + 128, :], NT))
        if step < 3:
            merged_grad(step + 1)
        send_back(0, step)

    def score_grads(step):
        grads = []
        for i in range(2):
            for m in range(2):
                p = 2 * rem(z + order[step], 4) + i
                value = jnp.concatenate([by_head(kvo[8 + p, 64 * m:64 * m + 64, :]),
                                         by_head(kvh[8 + p, 64 * m:64 * m + 64, :])], axis=0)
                gate_grad = mm(value, dm[step, m, 128 * i:128 * i + 128, :])
                grads.append((gate_grad * dsg[m, p]).astype(BF))
        return grads

    ready = score_grads(0)

    for a in range(2):
        for i in range(4):
            rows = slice(1024 * a + 256 * i, 1024 * a + 256 * i + 256)
            both = mm(um[0, rows, :], l4[0].reshape(128, 256), NT) + mm(
                um[1, rows, :], l4[1].reshape(128, 256), NT)
            ah[i % 2, a, i // 2] = both.astype(BF)
    swap = remote(ah.at[1 - core], ahx, ax_s, ax_r, sibling)
    swap.start()
    hid_forward(2)
    pending.append(swap)

    for step in range(4):
        for i in range(2):
            for m in range(2):
                p = 2 * rem(z + order[step], 4) + i
                keep(1, step, i, m, mm(ready[2 * i + m], q3[p]))
        if step < 3:
            ready = score_grads(step + 1)
        send_back(1, step)

    def node_step(h, step):
        g = rem(z + order[step], 4)
        for d in range(2):
            back_copy(h, step, d, True).wait_recv()
        total = (nown[h, step] + mm(scatter, nrecv[h, step].reshape(128, 256))).astype(BF)
        for c in range(2):
            nsnd[h, step, c] = total[:, 128 * c:128 * c + 128]
        if step < 3:
            for c in range(2):
                remote(nsnd.at[h, step, c], nrcv.at[h, group], na_s.at[h], na_r.at[h],
                       group_peer(2 * g + c)).start()
        else:
            remote(nsnd.at[h, 3, 1 - core], nrcv.at[h, group], na_s.at[h], na_r.at[h], sibling).start()
            sent(nrcv.at[h, 0:7], na_s.at[h], na_r.at[h])
            nrcv[h, group] = nsnd[h, 3, core]
        nt[:, pl.ds(pl.multiple_of(1024 * (1 - h) + g * 256, 256), 256)] = total

    swap.wait_recv()
    for a in range(2):
        for i in range(2):
            both = ah[core, a, i].astype(F32) + ahx[a, i].astype(F32)
            both = both.astype(BF).reshape(2, 4, 2, 16, 128)
            for to in range(4):
                ahs[to, a, i] = both[:, to]
    for k in (2, 1, 3):
        to = rem(x + k, 4)
        remote(ahs.at[to], ahr.at[x], ah_s, ah_r, (mem, band + 4 * (to - x))).start()
    sent(ahr.at[0:3], ah_s, ah_r)
    ahr[x] = ahs[x]

    for step in range(4):
        node_step(0, step)


    for step in range(4):
        node_step(1, step)

    received(ahr.at[0:3], ah_s, ah_r)
    both = jnp.sum(ahr[...].astype(F32), axis=0).astype(BF)
    for to in range(4):
        ahs2[to] = both[:, :, to % 2, to // 2]
    for k in range(1, 4):
        to = rem(y + k, 4)
        remote(ahs2.at[to], ahr2.at[y], ay_s, ay_r,
               (z * 2 + rem(to, 2), x * 4 + div(to, 2) * 2 + core)).start()
    sent(ahr2.at[0:3], ay_s, ay_r)
    ahr2[y] = ahs2[y]

    received(hgt.at[0], sib_s.at[3], sib_r.at[3])
    for a in range(3):
        received(hid_bulk(a), sib_s.at[a], sib_r.at[a])
    for h in range(2):
        received(nrcv.at[h, 0:7], na_s.at[h], na_r.at[h])
        node_cols = nrcv[h].reshape(1024, 128)
        for i in range(4):
            rows = slice(256 * i, 256 * i + 256)
            left = jnp.concatenate([hgt[j, rows, :] for j in range(8)], axis=1)
            kvp[h, :, i] = mm(left, node_cols).astype(BF).reshape(16, 16, 128)
        for k in range(1, 16):
            to = rem(plane + k, 16)
            remote(kvp.at[h, to], kvr.at[h, plane], rs_s.at[h], rs_r.at[h], plane_peer(to)).start()
        kvr[h, plane] = kvp[h, plane]

    for i in range(4):
        rows = slice(256 * i, 256 * i + 256)
        hg[:, rows] = mm(nt[...], kvw[rows, :], NT)
    hg_copy = pltpu.make_async_copy(hg, hg_hbm, out_sem)
    hg_copy.start()
    flush()

    def fin_send(part, sem):
        for k in (4, 5, 2, 3, 6, 7, 1):
            to = rem(group + k, 8)
            remote(fsnd.at[part, to], frcv.at[part, group], fin_s.at[sem], fin_r.at[sem],
                   group_peer(to)).start()
        bulk = frcv.at[part, 0:7]
        sent(bulk, fin_s.at[sem], fin_r.at[sem])

    received(ahr2.at[0:3], ay_s, ay_r)
    ah_sum = jnp.sum(ahr2[...].astype(F32), axis=0)
    for i in range(2):
        for c in range(2):
            at = (2 * i + core) * 2 + c
            other = (2 * i + 1 - core) * 2 + c
            for a in range(2):
                fsnd[2 + a, at] = ah_sum[a, i, 8 * c:8 * c + 8]
                fsnd[2 + a, other] = jnp.zeros((8, 128), F32)
    for part in (2, 3):
        fin_send(part, part)
        frcv[part, group] = fsnd[part, group]
    for h in range(2):
        received(kvr.at[h, 0:15], rs_s.at[h], rs_r.at[h])
        fsnd[h] = jnp.sum(kvr[h].astype(F32), axis=0).reshape(8, 8, 128)
        fin_send(h, h)
        frcv[h, group] = fsnd[h, group]
    for h in range(2):
        sent(kvr.at[h, 0:15], rs_s.at[h], rs_r.at[h])
    flush()
    hg_copy.wait()
    for part in (2, 3, 0, 1):
        received(frcv.at[part, 0:7], fin_s.at[part], fin_r.at[part])


def finish(hg, frcv, head, hg_out, kv_out, og_out, hd_out, headt, sem):
    copy = pltpu.make_async_copy(hg, hg_out, sem)
    copy.start()
    headt[...] = jnp.zeros_like(headt)
    headt[0:100, :] = head[...]
    for j in range(8):
        at = 128 * j
        kv_out[:, at:at + 128] = frcv[1, j] * (1.0 / DEVICES)
        kv_out[:, 1024 + at:1024 + at + 128] = frcv[0, j] * (1.0 / DEVICES)
    sums = jnp.sum(frcv[2:4], axis=1) * (1.0 / DEVICES)
    hd_out[...] = sums[1, :, 0:100]
    outer = sums[0]
    big = outer.astype(BF)
    small = (outer - big.astype(F32)).astype(BF)
    og_out[...] = mm(big, headt[...]) + mm(small, headt[...])
    copy.wait()


def shards(hidden, queries, kv_weight, out_weight, head_projection, initial_state, truth,
           latitude_weight, channel_loss_weight, sources, halo_rows):
    vmem = pl.BlockSpec(memory_space=pltpu.VMEM)
    hbm = pl.BlockSpec(memory_space=pl.ANY)
    dma = pltpu.SemaphoreType.DMA
    scratch = [
        ((100, 1024), BF), ((100, 256), F32), ((100, 256), F32), ((1, 256), F32), ((1, 100), F32),
        ((3, 256), jnp.int32), ((2, 32), jnp.int32),
        ((2, 4, 32, 1024), BF), ((8, 256, 128), BF), ((1024, 2048), BF), ((1024, 1024), BF),
        ((1024, 1024), BF), ((1024, 256), BF), ((1024, 128), BF), ((128, 1024), BF),
        ((8, 1024, 128), BF), ((2, 2, 32, 1024), BF), ((8, 128), jnp.int32), ((16, 128, 128), BF),
        ((16, 128, 128), BF), ((2, 8, 128, 128), BF),
        ((256, 256), F32), ((2, 8, 256, 256), BF), ((2, 8, 256, 256), F32), ((2, 2048, 256), BF),
        ((128, 256), F32), ((128, 256), F32), ((128, 256), F32), ((2, 128, 256), F32),
        ((16, 16, 256), F32), ((16, 16, 256), BF), ((2, 8, 16, 256), BF), ((2, 1024, 256), BF),
        ((4, 2, 256, 256), BF), ((2, 2, 2, 256, 128), BF), ((2, 2, 256, 128), BF),
        ((4, 2, 2, 2, 2, 16, 128), BF), ((4, 2, 2, 2, 2, 16, 128), BF),
        ((4, 2, 2, 16, 128), BF), ((4, 2, 2, 16, 128), BF),
        ((2, 4, 128, 256), F32), ((2, 2, 4, 2, 32, 256), BF), ((2, 4, 2, 2, 32, 256), BF),
        ((128, 2048), BF), ((2, 4, 2, 128, 128), BF), ((2, 8, 128, 128), BF),
        ((2, 16, 4, 16, 128), BF), ((2, 16, 4, 16, 128), BF), ((4, 8, 8, 128), F32),
        ((128, 1024), F32),
    ]
    sems = [(18,), (), (2,), (2,), (3,), (3,), (4,), (4,), (2,), (2,), (), (), (), (), (), (), (2, 4, 2),
            (2, 4, 2), (2,), (2,), (2,), (2,), (4,), (4,), (), ()]
    raw_hidden, raw_sums = pl.pallas_call(
        body,
        out_shape=[jax.ShapeDtypeStruct((128, 1024), F32), jax.ShapeDtypeStruct((4, 8, 8, 128), F32)],
        in_specs=[hbm] * 11,
        out_specs=[hbm, vmem],
        scratch_shapes=[pltpu.VMEM(shape, kind) for shape, kind in scratch] + [dma(n) for n in sems],
        compiler_params=pltpu.CompilerParams(
            collective_id=0, has_side_effects=True, vmem_limit_bytes=56 * 1024 * 1024),
    )(
        hidden.reshape(2, 2, 32, 1024), queries, kv_weight, out_weight, head_projection.T,
        initial_state, truth, latitude_weight.reshape(1, 256), channel_loss_weight.reshape(1, 100),
        sources, halo_rows,
    )
    hidden_grad, kv_grad, out_grad, head_grad = pl.pallas_call(
        finish,
        out_shape=[jax.ShapeDtypeStruct((128, 1024), F32), jax.ShapeDtypeStruct((8, 2048), F32),
                   jax.ShapeDtypeStruct((8, 1024), F32), jax.ShapeDtypeStruct((8, 100), F32)],
        in_specs=[vmem, vmem, vmem],
        out_specs=[hbm, vmem, vmem, vmem],
        scratch_shapes=[pltpu.VMEM((128, 1024), BF), dma(())],
    )(raw_hidden, raw_sums, head_projection.T)
    return hidden_grad.reshape(2, 64, 1024), kv_grad, out_grad, head_grad


def solution(mesh):
    placed = (
        P("member", "band", None),
        P("band", None),
        P(),
        P(),
        P(),
        P(None, "band"),
        P(None, "band"),
        P("band"),
        P(),
        P(None, "band"),
        P("band", None),
    )
    return jax.shard_map(
        shards,
        mesh=mesh,
        in_specs=placed,
        out_specs=(
            P("member", "band", None),
            P(("member", "band"), None),
            P(("member", "band"), None),
            P(("member", "band"), None),
        ),
        check_vma=False,
    )
```

time: 60.9 us -> 56.8 us (0.933)
  Pallas kernels: 60 us -> 55.8 us
    pallas_call x1, Pallas kernels: 57.4 us -> 53.2 us  [shards(): pl.pallas_call(body, out_shape=[jax.ShapeDtypeStruct((128, 1024), F32), j...]
where the time goes in v4:
time: 56.8 us; the launch traced here: 56.6 us
  Pallas kernels  55.8 us (98%)
  between operations  0.8 us (1%)
    pallas_call x1, Pallas kernels, shards(): pl.pallas_call(body, out_shape=[jax.ShapeDtypeStruct((128, 1024), F32), j...  53.2 us
    pallas_call x1, Pallas kernels, shards(): pl.pallas_call(finish, out_shape=[jax.ShapeDtypeStruct((128, 1024), F32),...  2.6 us

profile of v4, /device:TPU:1, one launch (start us, length us, event | category | flops | bytes accessed | tf_op | source)
XLA Modules:
  0.0 56.6 jit_solution(2896763785218493215)
XLA Ops:
  0.6 53.2 %shard_map.138 = (f32[128,1024]{1,0:T(8,128)}, f32[4,8,8,128]{3,2,1,0:T(8,128)}) custom-call(bf16[2,2,32,1024]{3,2,1,0:T(8,128)(2,1)} %bitcast.7, bf16[256,1024]{1,0:T(8,128)(2,1)} %q_hbm.1, bf16[1024,2048]{1,0:T(8,128)(2,1)} %kvw_hbm.1, bf16[1024,1024]{1,0:T(8,128)(2,1)} %ow_hbm.1, bf16[100,1024]{1,0:T(8,128)(2,1)} %bitcast.5, f32[100,256]{1,0:T(8,128)} %init_hbm.1, ...), custom_call_target="tpu_custom_call" | custom-call | tf_op jit(solution)/shard_map/pallas_call | solution.py:486
  53.9 2.6 %shard_map.139 = (f32[128,1024]{1,0:T(8,128)}, f32[8,2048]{1,0:T(8,128)}, f32[8,1024]{1,0:T(8,128)}, f32[8,100]{1,0:T(8,128)}) custom-call(f32[128,1024]{1,0:T(8,128)} %get-tuple-element.10.hg, f32[4,8,8,128]{3,2,1,0:T(8,128)} %get-tuple-element.11.frcv, bf16[100,1024]{1,0:T(8,128)(2,1)} %bitcast.6), custom_call_target="tpu_custom_call" | custom-call | tf_op jit(solution)/shard_map/pallas_call | solution.py:499

commit v5 on v4

--- a/solution.py
+++ b/solution.py
@@ -124,7 +124,7 @@
     for n in range(8):
         rows = slice(128 * n, 128 * n + 128)
         hgt[group, rows, :] = own[:, rows].T
-    pieces = (pl.ds(0, 512), pl.ds(512, 256), pl.ds(768, 256))
+    pieces = (pl.ds(0, 256), pl.ds(256, 256), pl.ds(512, 512))
 
     def hid_piece(a, j):
         return hgt.at[j, pieces[a]]
@@ -258,10 +258,10 @@
                 remote(lloc.at[pl.ds(2 * to, 2)], l4.at[:, mem], lg_s, lg_r, member_peer(to)).start()
     sent(lloc.at[0:14], lg_s, lg_r)
     hid_forward(1)
-    hid_send(2)
     for m in range(2):
         l4[m, mem] = lloc[2 * mem + m]
     received(lloc.at[0:14], lg_s, lg_r)
+    hid_send(2)
 
     for m in range(2):
         grad = l4[m].reshape(128, 256)
@@ -325,7 +325,6 @@
             ah[i % 2, a, i // 2] = both.astype(BF)
     swap = remote(ah.at[1 - core], ahx, ax_s, ax_r, sibling)
     swap.start()
-    hid_forward(2)
     pending.append(swap)
 
     for step in range(4):
@@ -369,21 +368,11 @@
 
     for step in range(4):
         node_step(0, step)
+    hid_forward(2)
 
 
     for step in range(4):
         node_step(1, step)
-
-    received(ahr.at[0:3], ah_s, ah_r)
-    both = jnp.sum(ahr[...].astype(F32), axis=0).astype(BF)
-    for to in range(4):
-        ahs2[to] = both[:, :, to % 2, to // 2]
-    for k in range(1, 4):
-        to = rem(y + k, 4)
-        remote(ahs2.at[to], ahr2.at[y], ay_s, ay_r,
-               (z * 2 + rem(to, 2), x * 4 + div(to, 2) * 2 + core)).start()
-    sent(ahr2.at[0:3], ay_s, ay_r)
-    ahr2[y] = ahs2[y]
 
     received(hgt.at[0], sib_s.at[3], sib_r.at[3])
     for a in range(3):
@@ -399,6 +388,18 @@
             to = rem(plane + k, 16)
             remote(kvp.at[h, to], kvr.at[h, plane], rs_s.at[h], rs_r.at[h], plane_peer(to)).start()
         kvr[h, plane] = kvp[h, plane]
+        if h:
+            continue
+        received(ahr.at[0:3], ah_s, ah_r)
+        both = jnp.sum(ahr[...].astype(F32), axis=0).astype(BF)
+        for to in range(4):
+            ahs2[to] = both[:, :, to % 2, to // 2]
+        for k in range(1, 4):
+            to = rem(y + k, 4)
+            remote(ahs2.at[to], ahr2.at[y], ay_s, ay_r,
+                   (z * 2 + rem(to, 2), x * 4 + div(to, 2) * 2 + core)).start()
+        sent(ahr2.at[0:3], ay_s, ay_r)
+        ahr2[y] = ahs2[y]
 
     for i in range(4):
         rows = slice(256 * i, 256 * i + 256)

time: 56.8 us -> 56.2 us (0.989)
  Pallas kernels: 55.8 us -> 55.2 us
    pallas_call x1, Pallas kernels: 53.2 us -> 52.6 us  [shards(): pl.pallas_call(body, out_shape=[jax.ShapeDtypeStruct((128, 1024), F32), j...]
where the time goes in v5:
time: 56.2 us; the launch traced here: 56 us
  Pallas kernels  55.2 us (98%)
  between operations  0.8 us (1%)
    pallas_call x1, Pallas kernels, shards(): pl.pallas_call(body, out_shape=[jax.ShapeDtypeStruct((128, 1024), F32), j...  52.6 us
    pallas_call x1, Pallas kernels, shards(): pl.pallas_call(finish, out_shape=[jax.ShapeDtypeStruct((128, 1024), F32),...  2.6 us

profile of v5, /device:TPU:1, one launch (start us, length us, event | category | flops | bytes accessed | tf_op | source)
XLA Modules:
  0.0 56.0 jit_solution(12755102240899453176)
XLA Ops:
  0.6 52.6 %shard_map.138 = (f32[128,1024]{1,0:T(8,128)}, f32[4,8,8,128]{3,2,1,0:T(8,128)}) custom-call(bf16[2,2,32,1024]{3,2,1,0:T(8,128)(2,1)} %bitcast.7, bf16[256,1024]{1,0:T(8,128)(2,1)} %q_hbm.1, bf16[1024,2048]{1,0:T(8,128)(2,1)} %kvw_hbm.1, bf16[1024,1024]{1,0:T(8,128)(2,1)} %ow_hbm.1, bf16[100,1024]{1,0:T(8,128)(2,1)} %bitcast.5, f32[100,256]{1,0:T(8,128)} %init_hbm.1, ...), custom_call_target="tpu_custom_call" | custom-call | tf_op jit(solution)/shard_map/pallas_call | solution.py:487
  53.2 2.6 %shard_map.139 = (f32[128,1024]{1,0:T(8,128)}, f32[8,2048]{1,0:T(8,128)}, f32[8,1024]{1,0:T(8,128)}, f32[8,100]{1,0:T(8,128)}) custom-call(f32[128,1024]{1,0:T(8,128)} %get-tuple-element.10.hg, f32[4,8,8,128]{3,2,1,0:T(8,128)} %get-tuple-element.11.frcv, bf16[100,1024]{1,0:T(8,128)(2,1)} %bitcast.6), custom_call_target="tpu_custom_call" | custom-call | tf_op jit(solution)/shard_map/pallas_call | solution.py:500

commit v6 on v5

--- a/solution.py
+++ b/solution.py
@@ -441,10 +441,20 @@
         received(frcv.at[part, 0:7], fin_s.at[part], fin_r.at[part])
 
 
-def finish(hg, frcv, head, hg_out, kv_out, og_out, hd_out, headt, sem):
-    copy = pltpu.make_async_copy(hg, hg_out, sem)
-    copy.start()
+def finish(hg_hbm, frcv_hbm, head_hbm, hg_out, kv_out, og_out, hd_out, hg, frcv, head, headt, sem, out_sem):
+    loads = [pltpu.make_async_copy(frcv_hbm, frcv, sem.at[4]),
+             pltpu.make_async_copy(head_hbm, head, sem.at[5])]
+    quarters = [pl.ds(32 * i, 32) for i in range(4)]
+    loads += [pltpu.make_async_copy(hg_hbm.at[q], hg.at[q], sem.at[i]) for i, q in enumerate(quarters)]
+    for copy in loads:
+        copy.start()
+    stores = [pltpu.make_async_copy(hg.at[q], hg_out.at[q], out_sem.at[i]) for i, q in enumerate(quarters)]
     headt[...] = jnp.zeros_like(headt)
+    for load, store in zip(loads[2:], stores):
+        load.wait()
+        store.start()
+    loads[0].wait()
+    loads[1].wait()
     headt[0:100, :] = head[...]
     for j in range(8):
         at = 128 * j
@@ -456,7 +466,8 @@
     big = outer.astype(BF)
     small = (outer - big.astype(F32)).astype(BF)
     og_out[...] = mm(big, headt[...]) + mm(small, headt[...])
-    copy.wait()
+    for copy in stores:
+        copy.wait()
 
 
 def shards(hidden, queries, kv_weight, out_weight, head_projection, initial_state, truth,
@@ -501,9 +512,10 @@
         finish,
         out_shape=[jax.ShapeDtypeStruct((128, 1024), F32), jax.ShapeDtypeStruct((8, 2048), F32),
                    jax.ShapeDtypeStruct((8, 1024), F32), jax.ShapeDtypeStruct((8, 100), F32)],
-        in_specs=[vmem, vmem, vmem],
+        in_specs=[hbm, hbm, hbm],
         out_specs=[hbm, vmem, vmem, vmem],
-        scratch_shapes=[pltpu.VMEM((128, 1024), BF), dma(())],
+        scratch_shapes=[pltpu.VMEM((128, 1024), F32), pltpu.VMEM((4, 8, 8, 128), F32),
+                        pltpu.VMEM((100, 1024), BF), pltpu.VMEM((128, 1024), BF), dma((6,)), dma((4,))],
     )(raw_hidden, raw_sums, head_projection.T)
     return hidden_grad.reshape(2, 64, 1024), kv_grad, out_grad, head_grad
 

time: 56.2 us -> 56.2 us (level)
  no operation moved by 1% of the time
where the time goes in v6:
time: 56.2 us; the launch traced here: 56 us
  Pallas kernels  55.2 us (98%)
  between operations  0.8 us (1%)
    pallas_call x1, Pallas kernels, shards(): pl.pallas_call(body, out_shape=[jax.ShapeDtypeStruct((128, 1024), F32), j...  52.6 us
    pallas_call x1, Pallas kernels, shards(): pl.pallas_call(finish, out_shape=[jax.ShapeDtypeStruct((128, 1024), F32),...  2.63 us

profile of v6, /device:TPU:1, one launch (start us, length us, event | category | flops | bytes accessed | tf_op | source)
XLA Modules:
  0.0 56.0 jit_solution(16410156813493431398)
XLA Ops:
  0.6 52.6 %shard_map.138 = (f32[128,1024]{1,0:T(8,128)}, f32[4,8,8,128]{3,2,1,0:T(8,128)}) custom-call(bf16[2,2,32,1024]{3,2,1,0:T(8,128)(2,1)} %bitcast.7, bf16[256,1024]{1,0:T(8,128)(2,1)} %q_hbm.1, bf16[1024,2048]{1,0:T(8,128)(2,1)} %kvw_hbm.1, bf16[1024,1024]{1,0:T(8,128)(2,1)} %ow_hbm.1, bf16[100,1024]{1,0:T(8,128)(2,1)} %bitcast.5, f32[100,256]{1,0:T(8,128)} %init_hbm.1, ...), custom_call_target="tpu_custom_call" | custom-call | tf_op jit(solution)/shard_map/pallas_call | solution.py:498
  53.2 2.6 %shard_map.139 = (f32[128,1024]{1,0:T(8,128)}, f32[8,2048]{1,0:T(8,128)}, f32[8,1024]{1,0:T(8,128)}, f32[8,100]{1,0:T(8,128)}) custom-call(f32[128,1024]{1,0:T(8,128)} %get-tuple-element.10.hg_hbm, f32[4,8,8,128]{3,2,1,0:T(8,128)} %get-tuple-element.11.frcv_hbm, bf16[100,1024]{1,0:T(8,128)(2,1)} %bitcast.6), custom_call_target="tpu_custom_call" | custom-call | tf_op jit(solution)/shard_map/pallas_call | solution.py:511

commit v7 on v6

--- a/solution.py
+++ b/solution.py
@@ -180,8 +180,8 @@
             cols = slice(256 * j, 256 * j + 256)
             owt[rows, cols] = ow[cols, rows].T
 
-    def project(rows, target):
-        for n in range(8):
+    def project(rows, target, parts=range(8)):
+        for n in parts:
             part = mm(rows, kvw[:, 256 * n:256 * n + 256]).astype(BF)
             target[2 * n] = part[:, :128]
             target[2 * n + 1] = part[:, 128:]
@@ -207,11 +207,13 @@
             vto[m, p] = by_head(kvo[8 + p, 64 * m:64 * m + 64, :]).T
     to_below.wait_recv()
     to_above.wait_recv()
-    project(ext[:, 2:4].reshape(128, 1024), kvh)
+    received_rows = ext[:, 2:4].reshape(128, 1024)
 
     my_rows = pl.ds(pl.multiple_of(mem * 16, 16), 16)
     for m in range(2):
         for p in range(8):
+            if m == 0 and p % 2 == 0:
+                project(received_rows, kvh, (p // 2, 4 + p // 2))
             gate = jnp.concatenate([gt[m, p, 0:128, :], gates(1, kvh, m, p)], axis=0)
             value = by_head(kvh[8 + p, 64 * m:64 * m + 64, :]).T
             value = jnp.concatenate([vto[m, p], value], axis=1)

time: 56.2 us -> 56.5 us (level)
  no operation moved by 1% of the time
where the time goes in v7:
time: 56.5 us; the launch traced here: 56.4 us
  Pallas kernels  55.6 us (98%)
  between operations  0.8 us (1%)
    pallas_call x1, Pallas kernels, shards(): pl.pallas_call(body, out_shape=[jax.ShapeDtypeStruct((128, 1024), F32), j...  52.9 us
    pallas_call x1, Pallas kernels, shards(): pl.pallas_call(finish, out_shape=[jax.ShapeDtypeStruct((128, 1024), F32),...  2.63 us

profile of v7, /device:TPU:1, one launch (start us, length us, event | category | flops | bytes accessed | tf_op | source)
XLA Modules:
  0.0 56.4 jit_solution(787514976989418407)
XLA Ops:
  0.6 52.9 %shard_map.138 = (f32[128,1024]{1,0:T(8,128)}, f32[4,8,8,128]{3,2,1,0:T(8,128)}) custom-call(bf16[2,2,32,1024]{3,2,1,0:T(8,128)(2,1)} %bitcast.7, bf16[256,1024]{1,0:T(8,128)(2,1)} %q_hbm.1, bf16[1024,2048]{1,0:T(8,128)(2,1)} %kvw_hbm.1, bf16[1024,1024]{1,0:T(8,128)(2,1)} %ow_hbm.1, bf16[100,1024]{1,0:T(8,128)(2,1)} %bitcast.5, f32[100,256]{1,0:T(8,128)} %init_hbm.1, ...), custom_call_target="tpu_custom_call" | custom-call | tf_op jit(solution)/shard_map/pallas_call | solution.py:500
  53.6 2.6 %shard_map.139 = (f32[128,1024]{1,0:T(8,128)}, f32[8,2048]{1,0:T(8,128)}, f32[8,1024]{1,0:T(8,128)}, f32[8,100]{1,0:T(8,128)}) custom-call(f32[128,1024]{1,0:T(8,128)} %get-tuple-element.10.hg_hbm, f32[4,8,8,128]{3,2,1,0:T(8,128)} %get-tuple-element.11.frcv_hbm, bf16[100,1024]{1,0:T(8,128)(2,1)} %bitcast.6), custom_call_target="tpu_custom_call" | custom-call | tf_op jit(solution)/shard_map/pallas_call | solution.py:513
